TPU v7x, 128 devices: a whole 4x4x4 slice. The times are simulated.
128 devices in a mesh: pool: 2 (over x_lo), pw: 64 (over z, x_hi, y, core).
Axes of the slice: x: 4 (x_hi: 2, x_lo: 2; x = x_hi * 2 + x_lo), y: 4, z: 4, core: 2. Of those that a mesh axis runs over, the one named last changes fastest.
Arguments:
- orbitals: float32 [2, 2, 2, 192, 192, 192], P('pool', None, None, 'pw'), may hold values from -6 to 6
- responses: float32 [2, 2, 2, 192, 192, 192], P('pool', None, None, 'pw'), may hold values from -6 to 6
- energies: float32 [2, 2], P('pool'), may hold values from -0.6 to 0.4
- weights: float32 [2], P('pool'), may hold values from 0.5 to 1.5
- potential: float32 [192, 192, 192], P(None, 'pw'), may hold values from -3 to 3
- perturbation: float32 [192, 192, 192], P(None, 'pw'), may hold values from 0.2 to 2
Outputs:
- new_responses: float32 [2, 2, 2, 192, 192, 192], P('pool', None, None, 'pw')
- response_density: float32 [192, 192, 192], P('pw')
All inputs are finite; a program needn't handle non-finite values.
Results may differ from a plain program's by a relative error of at most 0.0003.
Values sent between devices are 32-bit elements; how exact they have to be, the bound alone decides.
A program may use at most 128 MiB of HBM per device.

v0:
```python
import math

import jax
import jax.numpy as jnp
from jax import lax
from jax.sharding import PartitionSpec as P

RECIPROCAL_SQUARE = 0.023428


def tables(length):
    indices = jnp.arange(length, dtype=jnp.int32)
    angles = (indices[:, None] * indices[None, :] % length).astype(jnp.float32) * (
        2.0 * math.pi / length
    )
    factor = 1.0 / math.sqrt(length)
    return (jnp.cos(angles) * factor, jnp.sin(angles) * factor)


def apply_table(values, table_in, along_axis):
    rotated = jnp.tensordot(
        values, table_in, axes=((along_axis,), (0,)), precision=lax.Precision.HIGHEST
    )
    return jnp.moveaxis(rotated, -1, along_axis)


def transform(field_in, along_axis, cosine_table, sine_table, phase_sign):
    real_part = field_in[:, :, 0]
    imag_part = field_in[:, :, 1]
    real_cos = apply_table(real_part, cosine_table, along_axis)
    real_sin = apply_table(real_part, sine_table, along_axis)
    imag_cos = apply_table(imag_part, cosine_table, along_axis)
    imag_sin = apply_table(imag_part, sine_table, along_axis)
    return jnp.stack((real_cos - phase_sign * imag_sin, phase_sign * real_sin + imag_cos), axis=2)


def signed_freq(indices, length):
    return jnp.where(indices < length // 2, indices, indices - length).astype(jnp.float32)


def negated(values, along_axis):
    return jnp.roll(jnp.flip(values, along_axis), 1, along_axis)


def products(left_side, right_side):
    band_count = left_side.shape[0]
    highest = lax.Precision.HIGHEST
    left_real = left_side[:, 0].reshape(band_count, -1)
    left_imag = left_side[:, 1].reshape(band_count, -1)
    right_real = right_side[:, 0].reshape(band_count, -1)
    right_imag = right_side[:, 1].reshape(band_count, -1)
    real_sum = jnp.dot(left_real, right_real.T, precision=highest) + jnp.dot(
        left_imag, right_imag.T, precision=highest
    )
    imag_sum = jnp.dot(left_real, right_imag.T, precision=highest) - jnp.dot(
        left_imag, right_real.T, precision=highest
    )
    return (real_sum, imag_sum)


def body(orbitals, responses, energies, weights, potential, perturbation):
    length = orbitals.shape[-1]
    slab_rows = orbitals.shape[3]
    cosine_table, sine_table = tables(length)

    def to_space(field_in):
        return transform(
            transform(field_in, 4, cosine_table, sine_table, 1.0), 3, cosine_table, sine_table, 1.0
        )

    def finish_one(one_piece):
        return transform(one_piece, 2, cosine_table, sine_table, 1.0)

    orbital_space = finish_one(
        lax.all_to_all(to_space(orbitals), "pw", split_axis=4, concat_axis=3, tiled=True)
    )
    response_space = finish_one(
        lax.all_to_all(to_space(responses), "pw", split_axis=4, concat_axis=3, tiled=True)
    )
    partial_value = (
        2.0
        * weights[0]
        * jnp.sum(
            orbital_space[0, :, 0] * response_space[0, :, 0]
            + orbital_space[0, :, 1] * response_space[0, :, 1],
            axis=0,
        )
    )
    applied_space = potential * response_space + perturbation * orbital_space
    first_row = lax.axis_index("pw") * slab_rows
    row_freq = signed_freq(first_row + jnp.arange(slab_rows, dtype=jnp.int32), length)
    full_freq = signed_freq(jnp.arange(length, dtype=jnp.int32), length)
    kinetic = (
        0.5
        * RECIPROCAL_SQUARE
        * (
            row_freq[:, None, None] * row_freq[:, None, None]
            + full_freq[None, :, None] * full_freq[None, :, None]
            + full_freq[None, None, :] * full_freq[None, None, :]
        )
    )
    shifted = kinetic[None] - energies[0][:, None, None, None]
    direct = shifted[None, :, None] * responses
    sectioned = transform(
        transform(applied_space, 4, cosine_table, sine_table, -1.0),
        2,
        cosine_table,
        sine_table,
        -1.0,
    )
    residual = direct + transform(
        lax.all_to_all(sectioned, "pw", split_axis=3, concat_axis=4, tiled=True),
        3,
        cosine_table,
        sine_table,
        -1.0,
    )
    over_real, over_imag = lax.psum(products(orbitals[0], residual[0]), "pw")
    highest = lax.Precision.HIGHEST
    orbital_real = orbitals[0, :, 0]
    orbital_imag = orbitals[0, :, 1]
    combine_real = jnp.einsum(
        "mn,mxyz->nxyz", over_real, orbital_real, precision=highest
    ) - jnp.einsum("mn,mxyz->nxyz", over_imag, orbital_imag, precision=highest)
    combine_imag = jnp.einsum(
        "mn,mxyz->nxyz", over_imag, orbital_real, precision=highest
    ) + jnp.einsum("mn,mxyz->nxyz", over_real, orbital_imag, precision=highest)
    cell_count = float(length**3)
    projected = residual - jnp.stack((combine_real, combine_imag), axis=1)[None] / cell_count
    new_responses = responses - projected / (1.0 + kinetic)[None, None, None]
    summed = lax.psum(partial_value, "pool")
    mirrored = summed + negated(summed, 0)
    row_slab = lax.all_to_all(mirrored, "pw", split_axis=0, concat_axis=1, tiled=True)
    signsum = row_slab + negated(row_slab, 1)
    swapped = lax.all_to_all(signsum, "pw", split_axis=1, concat_axis=0, tiled=True)
    total_sym = signsum + jnp.transpose(swapped, (1, 0, 2))
    return (new_responses, total_sym / 8.0)


def solution(mesh):
    placed = (
        P("pool", None, None, "pw", None, None),
        P("pool", None, None, "pw", None, None),
        P("pool", None),
        P("pool"),
        P(None, "pw", None),
        P(None, "pw", None),
    )
    return jax.shard_map(
        body,
        mesh=mesh,
        in_specs=placed,
        out_specs=(P("pool", None, None, "pw", None, None), P("pw", None, None)),
        check_vma=False,
    )
```

profile of v0, /device:TPU:0, one launch (start us, length us, event | category | flops | bytes accessed | tf_op | source)
XLA Modules:
  0.0 585.2 jit_solution(10836431347195345888)
XLA Ops:
  7.2 4.6 fusion.22
  32.0 12.3 %all-to-all-start = ((f32[1,2,2,3,192,192]{5,2,3,1,0,4:T(2,128)}), f32[1,2,2,3,192,192]{5,2,3,1,0,4:T(2,128)}, u32[]{:S(2)}, u32[]{:S(2)}) async-start(f32[1,2,2,3,192,192]{5,2,3,1,0,4:T(2,128)} %copy.169), calls=%async_computation | async-start | bytes 4718592 | tf_op jit(solution)/shard_map/all_to_all | solution.py:78
  66.1 4.5 copy.181
  70.6 6.0 %all-to-all-done = f32[1,2,2,3,192,192]{5,2,3,1,0,4:T(2,128)} async-done(((f32[1,2,2,3,192,192]{5,2,3,1,0,4:T(2,128)}), f32[1,2,2,3,192,192]{5,2,3,1,0,4:T(2,128)}, u32[]{:S(2)}, u32[]{:S(2)}) %all-to-all-start) | async-done | bytes 1769504 | tf_op jit(solution)/shard_map/all_to_all | solution.py:78
  76.6 5.6 all-to-all-start.1
  100.6 14.4 %all-to-all-done.1 = f32[1,2,2,3,192,192]{5,2,3,1,0,4:T(2,128)} async-done(((f32[1,2,2,3,192,192]{5,2,3,1,0,4:T(2,128)}), f32[1,2,2,3,192,192]{5,2,3,1,0,4:T(2,128)}, u32[]{:S(2)}, u32[]{:S(2)}) %all-to-all-start.1) | async-done | bytes 1769504 | tf_op jit(solution)/shard_map/all_to_all | solution.py:75
  165.4 15.5 %all-reduce.3.cloned.1.call-done = f32[192,3,192]{0,2,1:T(8,128)} async-done(((f32[192,3,192]{0,2,1:T(8,128)}), f32[192,3,192]{0,2,1:T(8,128)}) %all-reduce.3.cloned.1.call-update) | async-done | bytes 442384 | tf_op jit(solution)/shard_map/psum | solution.py:131
  182.9 7.0 %reverse.4 = f32[256,3,192]{0,2,1:T(8,128)} reverse(f32[256,3,192]{0,2,1:T(8,128)} %bitcast.362), dimensions={0} | reverse | bytes 1179648
  194.6 10.6 %all-to-all-start.3 = ((f32[192,3,192]{2,1,0:T(4,128)}), f32[192,3,192]{2,1,0:T(4,128)}, u32[]{:S(2)}, u32[]{:S(2)}) async-start(f32[192,3,192]{2,1,0:T(4,128)} %copy.213), calls=%async_computation.3 | async-start | bytes 1572864 | tf_op jit(solution)/shard_map/all_to_all | solution.py:133
  213.6 8.2 %all-to-all-done.3 = f32[192,3,192]{2,1,0:T(4,128)} async-done(((f32[192,3,192]{2,1,0:T(4,128)}), f32[192,3,192]{2,1,0:T(4,128)}, u32[]{:S(2)}, u32[]{:S(2)}) %all-to-all-start.3) | async-done | bytes 442400 | tf_op jit(solution)/shard_map/all_to_all | solution.py:133
  228.8 6.8 %slice.95 = f32[3,191,192]{2,1,0:T(8,128)} reverse(f32[3,191,192]{2,1,0:T(8,128)} %slice.111), dimensions={1} | reverse | bytes 880128 | tf_op jit(solution)/shard_map/jit(_roll_static)/slice | solution.py:42
  239.1 5.6 all-to-all-start.4
  253.7 4.6 copy.194
  261.2 8.0 %all-to-all-start.2 = ((f32[1,2,2,192,3,192]{5,2,4,1,0,3:T(2,128)}), f32[1,2,2,192,3,192]{5,2,4,1,0,3:T(2,128)}, u32[]{:S(2)}, u32[]{:S(2)}) async-start(f32[1,2,2,192,3,192]{5,2,4,1,0,3:T(2,128)} %copy.194), calls=%async_computation.2 | async-start | bytes 4718592 | tf_op jit(solution)/shard_map/all_to_all | solution.py:112
  282.0 20.0 %all-to-all-done.2 = f32[1,2,2,192,3,192]{5,2,4,1,0,3:T(2,128)} async-done(((f32[1,2,2,192,3,192]{5,2,4,1,0,3:T(2,128)}), f32[1,2,2,192,3,192]{5,2,4,1,0,3:T(2,128)}, u32[]{:S(2)}, u32[]{:S(2)}) %all-to-all-start.2) | async-done | bytes 1769504 | tf_op jit(solution)/shard_map/all_to_all | solution.py:112
  328.5 12.8 %convolution_bitcast_fusion = f32[2,2]{1,0:T(2,128)S(1)} fusion(f32[2,3,192,192]{3,0,2,1:T(2,128)} %copy.200, f32[2,2,3,192,192]{4,0,3,2,1:T(2,128)} %bitcast.358), kind=kOutput, calls=%fused_computation.91 | convolution fusion | flops 5308416 | bytes 2359312 | tf_op jit(solution)/shard_map/dot_general | solution.py:55
  341.3 11.2 %convolution_bitcast_fusion.2 = f32[2,2]{1,0:T(2,128)S(1)} fusion(f32[2,3,192,192]{3,0,2,1:T(2,128)S(1)} %copy-done.30, f32[2,2,3,192,192]{4,0,3,2,1:T(2,128)S(1)} %bitcast.359), kind=kOutput, calls=%fused_computation.93 | convolution fusion | flops 5308416 | bytes 2359312 | tf_op jit(solution)/shard_map/dot_general | solution.py:52
  352.5 11.0 %fusion.53 = f32[2,2]{0,1:T(2,128)S(1)} fusion(f32[2,2]{1,0:T(2,128)S(1)} %convolution_bitcast_fusion, f32[2,3,192,192]{3,0,2,1:T(2,128)S(1)} %copy-done.30, f32[2,2,3,192,192]{4,0,3,2,1:T(2,128)S(1)} %bitcast.360), kind=kOutput, calls=%fused_computation.98 | convolution fusion | flops 5308420 | bytes 2360336 | tf_op jit(solution)/shard_map/dot_general | solution.py:55
  363.6 11.2 %fusion.51 = f32[2,2]{0,1:T(2,128)S(1)} fusion(f32[2,2]{1,0:T(2,128)S(1)} %convolution_bitcast_fusion.2, f32[2,3,192,192]{3,0,2,1:T(2,128)S(1)} %copy-done.29, f32[2,2,3,192,192]{4,0,3,2,1:T(2,128)S(1)} %bitcast.361), kind=kOutput, calls=%fused_computation.96 | convolution fusion | flops 5308420 | bytes 2360336 | tf_op jit(solution)/shard_map/dot_general | solution.py:52
  375.7 164.4 %all-reduce = (f32[2,2]{0,1:T(2,128)S(1)}, f32[2,2]{0,1:T(2,128)S(1)}) all-reduce(f32[2,2]{0,1:T(2,128)S(1)} %fusion.53, f32[2,2]{0,1:T(2,128)S(1)} %fusion.51), channel_id=1, replica_groups=mesh['pool'=2,'pw'=64] {'pw'}, use_global_device_ids=true, to_apply=%region_1.2 | all-reduce | flops 8 | bytes 64 | tf_op jit(solution)/shard_map/psum | solution.py:118
  540.1 5.1 fusion.54
  545.2 5.1 fusion.56
  550.3 5.1 fusion.58
  555.3 5.1 fusion.60
  (163 shorter events, 205.0 us)
Async XLA Ops:
  7.2 4.6 copy-start.1
  32.0 12.3 %copy-start = (f32[1,2,2,3,192,192]{5,4,3,2,1,0:T(8,128)S(1)}, f32[1,2,2,3,192,192]{5,4,3,2,1,0:T(8,128)}, u32[]{:S(2)}) copy-start(f32[1,2,2,3,192,192]{5,4,3,2,1,0:T(8,128)} %param.6) | copy-start | bytes 5308420
  32.0 44.7 %all-to-all-start = ((f32[1,2,2,3,192,192]{5,2,3,1,0,4:T(2,128)}), f32[1,2,2,3,192,192]{5,2,3,1,0,4:T(2,128)}, u32[]{:S(2)}, u32[]{:S(2)}) async-start(f32[1,2,2,3,192,192]{5,2,3,1,0,4:T(2,128)} %copy.169), calls=%async_computation | async-start | bytes 4718592 | tf_op jit(solution)/shard_map/all_to_all | solution.py:78
  70.6 12.4 %copy-start.31 = (f32[192,3,192]{2,0,1:T(8,128)S(1)}, f32[192,3,192]{2,0,1:T(8,128)}, u32[]{:S(2)}) copy-start(f32[192,3,192]{2,0,1:T(8,128)} %param.10) | copy-start | bytes 1327108
  76.6 38.4 %all-to-all-start.1 = ((f32[1,2,2,3,192,192]{5,2,3,1,0,4:T(2,128)}), f32[1,2,2,3,192,192]{5,2,3,1,0,4:T(2,128)}, u32[]{:S(2)}, u32[]{:S(2)}) async-start(f32[1,2,2,3,192,192]{5,2,3,1,0,4:T(2,128)} %copy.181), calls=%async_computation.1 | async-start | bytes 4718592 | tf_op jit(solution)/shard_map/all_to_all | solution.py:75
  82.2 98.7 %all-reduce.3.cloned.1.call-start = ((), (), s32[]{:S(2)}) async-start(), calls=%async_computation.5 | async-start | bytes 1179648 | tf_op jit(solution)/shard_map/psum | solution.py:131
  136.5 3.3 copy-start.22
  139.7 4.0 copy-start.14
  143.7 3.2 copy-start.17
  151.1 6.2 %copy-start.2 = (f32[1,2,2,192,3,192]{3,5,4,1,2,0:T(8,128)}, f32[1,2,2,192,3,192]{3,5,4,1,2,0:T(8,128)S(1)}, u32[]{:S(2)}) copy-start(f32[1,2,2,192,3,192]{3,5,4,1,2,0:T(8,128)S(1)} %fusion) | copy-start | bytes 5308420
  194.6 27.2 %all-to-all-start.3 = ((f32[192,3,192]{2,1,0:T(4,128)}), f32[192,3,192]{2,1,0:T(4,128)}, u32[]{:S(2)}, u32[]{:S(2)}) async-start(f32[192,3,192]{2,1,0:T(4,128)} %copy.213), calls=%async_computation.3 | async-start | bytes 1572864 | tf_op jit(solution)/shard_map/all_to_all | solution.py:133
  205.3 4.0 copy-start.3
  239.1 22.2 %all-to-all-start.4 = ((f32[3,192,192]{2,0,1:T(4,128)}), f32[3,192,192]{2,0,1:T(4,128)}, u32[]{:S(2)}, u32[]{:S(2)}) async-start(f32[3,192,192]{2,0,1:T(4,128)} %copy.216), calls=%async_computation.4 | async-start | bytes 1572864 | tf_op jit(solution)/shard_map/all_to_all | solution.py:135
  244.7 4.4 copy-start.21
  261.2 40.8 %all-to-all-start.2 = ((f32[1,2,2,192,3,192]{5,2,4,1,0,3:T(2,128)}), f32[1,2,2,192,3,192]{5,2,4,1,0,3:T(2,128)}, u32[]{:S(2)}, u32[]{:S(2)}) async-start(f32[1,2,2,192,3,192]{5,2,4,1,0,3:T(2,128)} %copy.194), calls=%async_computation.2 | async-start | bytes 4718592 | tf_op jit(solution)/shard_map/all_to_all | solution.py:112
  328.5 12.8 %copy-start.27 = (f32[1,2,2,3,192,192]{5,1,4,3,2,0:T(2,128)S(1)}, f32[1,2,2,3,192,192]{5,1,4,3,2,0:T(2,128)}, u32[]{:S(2)}) copy-start(f32[1,2,2,3,192,192]{5,1,4,3,2,0:T(2,128)} %copy.275) | copy-start | bytes 5308420
  328.5 12.8 %copy-start.30 = (f32[2,3,192,192]{3,0,2,1:T(2,128)S(1)}, f32[2,3,192,192]{3,0,2,1:T(2,128)}, u32[]{:S(2)}) copy-start(f32[2,3,192,192]{3,0,2,1:T(2,128)} %copy.201) | copy-start | bytes 2654212
  352.5 11.0 %copy-start.29 = (f32[2,3,192,192]{3,0,2,1:T(2,128)S(1)}, f32[2,3,192,192]{3,0,2,1:T(2,128)}, u32[]{:S(2)}) copy-start(f32[2,3,192,192]{3,0,2,1:T(2,128)} %copy.200) | copy-start | bytes 2654212
  363.5 11.2 %copy-start.19 = (f32[3,192,192]{2,1,0:T(8,128)S(1)}, f32[3,192,192]{2,1,0:T(8,128)}, u32[]{:S(2)}) copy-start(f32[3,192,192]{2,1,0:T(8,128)} %copy-done.18) | copy-start | bytes 1327108
  363.5 11.2 %copy-start.28 = (f32[192,3,192]{2,0,1:T(8,128)S(1)}, f32[192,3,192]{2,0,1:T(8,128)}, u32[]{:S(2)}) copy-start(f32[192,3,192]{2,0,1:T(8,128)} %all_to_all.84) | copy-start | bytes 1327108
  374.8 165.3 %copy-start.6 = (f32[2,3,192,192]{3,2,1,0:T(8,128)S(1)}, f32[2,3,192,192]{3,2,1,0:T(8,128)}, u32[]{:S(2)}) copy-start(f32[2,3,192,192]{3,2,1,0:T(8,128)} %get-tuple-element.12) | copy-start | bytes 2654212
  545.2 5.1 copy-start.5
  569.3 3.0 copy-start.12
  569.3 3.2 copy-start.26
  (17 other events, 30.2 us)
Sparse Core Ops, SparseCore 0:
  147.9 32.8 all-reduce.2
where the time goes:
time: 597 us; the launch traced here: 585 us
  matrix products  168 us (28%)
  blocking collectives  164 us (27%)
  local copies, waits for them, and re-layouts  110 us (18%)
  waiting for transfers between devices  67.1 us (11%)
  starting transfers between devices  42.1 us (7%)
  other arithmetic  17.8 us (3%)
  between operations  15.8 us (3%)
    psum x1, blocking collectives, body(): over_real, over_imag = lax.psum(products(orbitals[0], residual[0]), 'pw')  164 us
    dot_general x36, matrix products, apply_table(): jnp.tensordot(values, table_in, axes=((along_axis,), (0,)), precision=lax...  102 us
    unnamed x81, local copies, waits for them, and re-layouts  40.7 us
    all_to_all x1, waiting for transfers between devices, body(): lax.all_to_all(sectioned, 'pw', split_axis=3, concat_axis=4, tiled=True)  20 us
    psum x1, waiting for transfers between devices, body(): summed = lax.psum(partial_value, 'pool')  15.5 us
    all_to_all x1, waiting for transfers between devices, body(): lax.all_to_all(to_space(orbitals), 'pw', split_axis=4, concat_axis=3, til...  14.4 us
    dot_general x1, matrix products, products(): jnp.dot(left_imag, right_real.T, precision=highest)  12.8 us
    all_to_all x1, starting transfers between devices, body(): lax.all_to_all(to_space(responses), 'pw', split_axis=4, concat_axis=3, ti...  12.3 us
  transfers between devices with their start and end apart: 6, of which 6 were waited for; matrix products, arithmetic and copies ran while one was open for 16% of the time, Pallas kernels for 0%

commit v1 on v0

v1 whole, which is shorter than its diff:
```python
import functools
import math

import jax
import jax.numpy as jnp
import ml_dtypes
import numpy as np
from jax import lax
from jax.experimental import pallas as pl
from jax.experimental.pallas import tpu as pltpu
from jax.sharding import PartitionSpec as P

RECIPROCAL_SQUARE = 0.023428
G = 192
W = 64
R = 3
H = 104
BLOCKS = 27
MESH = pl.DeviceIdType.MESH
F32 = jnp.float32
BF16 = jnp.bfloat16


def halves(table):
    high = table.astype(ml_dtypes.bfloat16)
    low = (table - high.astype(np.float64)).astype(ml_dtypes.bfloat16)
    return [high, low]


def tables():
    index = np.arange(G)
    angles = (np.outer(index, index) % G) * (2.0 * math.pi / G)
    cosine = np.cos(angles) / math.sqrt(G)
    sine = np.sin(angles) / math.sqrt(G)
    spread = np.array([R * (s % W) + s // W for s in range(G)])

    def packed(left, right):
        return np.concatenate(
            (left[:, :128], right[:, :128], left[:, 128:], right[:, 128:]), axis=1
        )

    out_left = np.concatenate((cosine[spread], sine[spread]), axis=0)
    in_left = np.concatenate((cosine[:, spread], sine[:, spread]), axis=0)
    right_real = packed(cosine, sine)
    right_imag = packed(-sine, cosine)
    back_real = packed(cosine, -sine)
    back_imag = packed(sine, cosine)
    back = np.concatenate(
        (back_real[:128], back_imag[:128], back_real[128:], back_imag[128:]), axis=0
    )
    fold = np.zeros((H, G))
    unfold = np.zeros((G, H))
    merge = np.zeros((G, G))
    expand = np.zeros((G, H))
    for a in range(H):
        fold[a, a] += 1.0
        fold[a, -a % G] += 1.0
    for s in range(G):
        a = spread[s]
        unfold[s, min(a, G - a)] = 1.0
        merge[a, s] += 1.0
        merge[-a % G, s] += 1.0
        expand[s, min(s, G - s)] = 1.0
    held = []
    for table in (right_real, right_imag, out_left, in_left, back):
        held += halves(table)
    return held + [m.astype(ml_dtypes.bfloat16) for m in (fold, unfold, merge, expand)]


def split(values):
    high = values.astype(BF16)
    return high, (values - high.astype(F32)).astype(BF16)


def dot(left, right):
    return jnp.dot(left, right, preferred_element_type=F32)


def table_left(high, low, values):
    top, rest = split(values)
    return dot(high, top) + (dot(high, rest) + dot(low, top))


def table_right(values, high, low):
    top, rest = split(values)
    return dot(top, high) + (dot(rest, high) + dot(top, low))


def exact_left(table, values):
    top, rest = split(values)
    last = (values - top.astype(F32) - rest.astype(F32)).astype(BF16)
    return dot(table, top) + (dot(table, rest) + dot(table, last))


def swap64(values):
    return pltpu.roll(values, 64, axis=1)


def lane_sign():
    return jnp.where(lax.broadcasted_iota(jnp.int32, (1, 128), 1) < 64, -1.0, 1.0).astype(F32)


def spin(product, sign):
    cos_part, sin_part = product[:G], product[G:]
    return (
        cos_part[:, :128] - sign * sin_part[:, 128:256],
        cos_part[:, 128:256] + sign * sin_part[:, :128],
        cos_part[:, 256:] + (sign * lane_sign()) * swap64(sin_part[:, 256:]),
    )


def rows_of(start, count):
    return pl.ds(pl.multiple_of(start, 8), count)


def tiles_at(view, start):
    return jnp.concatenate([view[rows_of(start + t * G, G), :] for t in range(3)], axis=1)


def row_sums(values):
    total = values[0:8]
    for s in range(8, G, 8):
        total = total + values[s : s + 8]
    return total


def squared_freq(index):
    freq = jnp.where(index < G // 2, index, index - G).astype(F32)
    return freq * freq


def kinetic_plane(row):
    plane = squared_freq(lax.broadcasted_iota(jnp.int32, (G, G), 0))
    plane = plane + squared_freq(lax.broadcasted_iota(jnp.int32, (G, G), 1))
    return (0.5 * RECIPROCAL_SQUARE) * (squared_freq(row) + plane)


def kernel(
    orb_hbm, resp_hbm, pot_hbm, pert_hbm, energies, weights, *refs
):
    table_hbm = refs[:14]
    new_hbm, dens_hbm = refs[14:16]
    tables_in = refs[16:30]
    (
        raw, pot, pert, out_a, in_a, out_r, in_r, orb_space, app_space, dens,
        fold_mine, fold_other, fold_sum, fold_mirror, spread_out, spread_in,
        sums, sums_g, row_out, row_in, new_buf, dens_buf,
        load_sem, table_sem, send_a, recv_a, send_r, recv_r, send_d, recv_d, store_sem,
    ) = refs[30:]
    (wr_h, wr_l, wi_h, wi_l, ol_h, ol_l, il_h, il_l, bk_h, bk_l, fold, unfold, merge, expand) = tables_in

    me = lax.axis_index("pw")
    pool = lax.axis_index("pool")

    def load_table(k):
        return pltpu.make_async_copy(table_hbm[k], tables_in[k], table_sem.at[k])

    def load_unit(u):
        source = orb_hbm if u % 2 == 0 else resp_hbm
        return pltpu.make_async_copy(source.at[0, u // 2], raw.at[u], load_sem.at[u])

    loads_pot = pltpu.make_async_copy(pot_hbm, pot, load_sem.at[4])
    loads_pert = pltpu.make_async_copy(pert_hbm, pert, load_sem.at[5])
    for k in range(4):
        load_table(k).start()
    load_unit(0).start()
    for k in range(4, 6):
        load_table(k).start()
    for u in range(1, 4):
        load_unit(u).start()
    for k in range(6, 14):
        load_table(k).start()
    loads_pot.start()
    loads_pert.start()

    barrier = pltpu.get_barrier_semaphore()

    def peer_at(k):
        return me ^ (1 + (k * 37 + 11) % (W - 1))

    @pl.loop(0, W - 1)
    def _(k):
        pl.semaphore_signal(barrier, inc=1, device_id={"pw": peer_at(k)}, device_id_type=MESH)

    pl.semaphore_signal(barrier, inc=1, device_id={"pool": 1 - pool}, device_id_type=MESH)

    out_a_rows = out_a.reshape(4 * BLOCKS * W, 128)
    in_a_rows = in_a.reshape(4 * BLOCKS * W, 128)
    out_r_rows = out_r.reshape(2 * BLOCKS * W, 128)
    in_r_rows = in_r.reshape(2 * BLOCKS * W, 128)
    spread_out_rows = spread_out.reshape(15 * W, 128)
    spread_in_rows = spread_in.reshape(15 * W, 128)
    row_in_rows = row_in.reshape(W, 128)

    for k in range(6):
        load_table(k).wait()

    for u in range(4):
        load_unit(u).wait()

        @pl.loop(0, R)
        def _(i):
            planes = table_right(raw[u, 0, i], wr_h[...], wr_l[...]) + table_right(
                raw[u, 1, i], wi_h[...], wi_l[...]
            )
            parts = spin(table_left(ol_h[...], ol_l[...], planes), 1.0)
            for j in range(R):
                for t in range(3):
                    start = (u * BLOCKS + (j * 3 + t) * R + i) * W
                    out_a_rows[rows_of(start, W), :] = parts[t][j * W : (j + 1) * W]

        if u == 0:
            pl.semaphore_wait(barrier, W)

        @pl.loop(0, W - 1)
        def _(k):
            peer = peer_at(k)
            pltpu.make_async_remote_copy(
                src_ref=out_a.at[u, :, peer],
                dst_ref=in_a.at[u, :, me],
                send_sem=send_a.at[u],
                recv_sem=recv_a.at[u],
                device_id={"pw": peer},
                device_id_type=MESH,
            ).start()

        pltpu.make_async_copy(out_a.at[u, :, me], in_a.at[u, :, me], load_sem.at[6 + u]).start()

    for k in range(6, 14):
        load_table(k).wait()

    sums_g[...] = jnp.zeros_like(sums_g)

    @pl.loop(0, R)
    def _(i):
        kinetic = kinetic_plane(R * me + i)
        for n in range(2):
            shifted = kinetic - energies[0, n]
            real = shifted * raw[2 * n + 1, 0, i]
            imag = shifted * raw[2 * n + 1, 1, i]
            for m in range(2):
                left_real, left_imag = raw[2 * m, 0, i], raw[2 * m, 1, i]
                at = (m * 2 + n) * 2
                sums_g[at] += row_sums(left_real * real + left_imag * imag)
                sums_g[at + 1] += row_sums(left_real * imag - left_imag * real)

    loads_pot.wait()
    loads_pert.wait()
    sums[...] = jnp.zeros_like(sums)

    for n in range(2):
        for u in (2 * n, 2 * n + 1):
            landed = in_a.at[u, :, pl.ds(0, W - 1)]
            pltpu.make_async_copy(landed, landed, recv_a.at[u]).wait()
            pltpu.make_async_copy(out_a.at[u, :, me], in_a.at[u, :, me], load_sem.at[6 + u]).wait()

        @pl.loop(0, R)
        def _(j):
            at = j * 3 * G
            first = 2 * n * BLOCKS * W
            second = (2 * n + 1) * BLOCKS * W
            orb = spin(table_left(il_h[...], il_l[...], tiles_at(in_a_rows, first + at)), 1.0)
            resp = spin(table_left(il_h[...], il_l[...], tiles_at(in_a_rows, second + at)), 1.0)
            pot_top = pot[j, :, 0:128]
            pert_top = pert[j, :, 0:128]
            pot_end = jnp.concatenate((pot[j, :, 128:G], pot[j, :, 128:G]), axis=1)
            pert_end = jnp.concatenate((pert[j, :, 128:G], pert[j, :, 128:G]), axis=1)
            app = (
                pot_top * resp[0] + pert_top * orb[0],
                pot_top * resp[1] + pert_top * orb[1],
                pot_end * resp[2] + pert_end * orb[2],
            )
            ends = orb[2] * resp[2]
            density = (2.0 * weights[0]) * jnp.concatenate(
                (orb[0] * resp[0] + orb[1] * resp[1], ends + swap64(ends)), axis=1
            )

            def overlap(left, right, slot):
                sums[slot] += row_sums(left[0] * right[0] + left[1] * right[1] + left[2] * right[2])
                sums[slot + 1] += row_sums(
                    left[0] * right[1]
                    - left[1] * right[0]
                    - lane_sign() * left[2] * swap64(right[2])
                )

            if n == 0:
                overlap(orb, app, 0)
                dens[j] = density
                for t in range(3):
                    orb_space[j, t] = orb[t]
                    app_space[j, t] = app[t]
            else:
                dens[j] = dens[j] + density
                orb_first = [orb_space[j, t] for t in range(3)]
                app_first = [app_space[j, t] for t in range(3)]
                overlap(orb_first, app, 2)
                overlap(orb, app_first, 4)
                overlap(orb, app, 6)
            product = table_left(ol_h[...], ol_l[...], jnp.concatenate(app, axis=1))
            turned = jnp.concatenate(spin(product, -1.0), axis=1)
            back = table_right(turned, bk_h[...], bk_l[...])
            for i in range(R):
                for t in range(3):
                    start = (n * BLOCKS + (i * 3 + t) * R + j) * W
                    out_r_rows[rows_of(start, W), :] = back[
                        i * W : (i + 1) * W, t * 128 : (t + 1) * 128
                    ]

        if n == 1:
            low = lax.broadcasted_iota(jnp.int32, (1, 128), 1) < 64
            strips = (
                dens[0, :, 0:128],
                dens[0, :, 128:256],
                dens[1, :, 0:128],
                dens[2, :, 0:128],
                jnp.where(low, dens[1, :, 128:256], dens[2, :, 128:256]),
            )
            folded = exact_left(fold[...], jnp.concatenate(strips, axis=1))
            for t in range(5):
                fold_mine[t] = folded[:, t * 128 : (t + 1) * 128]
            pool_copy = pltpu.make_async_remote_copy(
                src_ref=fold_mine,
                dst_ref=fold_other,
                send_sem=send_d.at[0],
                recv_sem=recv_d.at[0],
                device_id={"pool": 1 - pool},
                device_id_type=MESH,
            )
            pool_copy.start()
            lane = lax.broadcasted_iota(jnp.int32, (1, 128), 1)
            row = jnp.zeros((1, 128), F32)
            for k in range(8):
                one = jnp.sum(sums[k], keepdims=True) + jnp.sum(sums_g[k], keepdims=True)
                row = jnp.where(lane == k, one, row)
            row_out[...] = row
            row_in[me] = row

        @pl.loop(0, W - 1)
        def _(k):
            peer = peer_at(k)
            pltpu.make_async_remote_copy(
                src_ref=out_r.at[n, :, peer],
                dst_ref=in_r.at[n, :, me],
                send_sem=send_r.at[n],
                recv_sem=recv_r.at[n],
                device_id={"pw": peer},
                device_id_type=MESH,
            ).start()
            if n == 1:
                pltpu.make_async_remote_copy(
                    src_ref=row_out,
                    dst_ref=row_in.at[me],
                    send_sem=send_r.at[2],
                    recv_sem=recv_r.at[2],
                    device_id={"pw": peer},
                    device_id_type=MESH,
                ).start()

        pltpu.make_async_copy(out_r.at[n, :, me], in_r.at[n, :, me], load_sem.at[10 + n]).start()

    pool_copy.wait()
    for t in range(5):
        fold_sum[t] = fold_mine[t] + fold_other[t]
    whole = exact_left(unfold[...], jnp.concatenate([fold_sum[t] for t in range(5)], axis=1))
    for t in range(5):
        spread_out_rows[pl.ds(t * G, G), :] = whole[:, t * 128 : (t + 1) * 128]

    opposite = (W - me) % W
    alone = opposite == me

    def mirror_first():
        return pltpu.make_async_remote_copy(
            src_ref=fold_sum.at[pl.ds(0, 2)],
            dst_ref=fold_mirror.at[pl.ds(0, 2)],
            send_sem=send_d.at[2],
            recv_sem=recv_d.at[2],
            device_id={"pw": opposite},
            device_id_type=MESH,
        )

    mirror_rest = pltpu.make_async_remote_copy(
        src_ref=fold_sum.at[pl.ds(2, 3)],
        dst_ref=fold_mirror.at[pl.ds(2, 3)],
        send_sem=send_d.at[3],
        recv_sem=recv_d.at[3],
        device_id={"pw": W - 1 - me},
        device_id_type=MESH,
    )
    mirror_rest.start()

    @pl.when(jnp.logical_not(alone))
    def _():
        mirror_first().start()

    @pl.when(alone)
    def _():
        for t in range(2):
            fold_mirror[t] = fold_sum[t]

    @pl.loop(0, W - 1)
    def _(k):
        peer = peer_at(k)
        pltpu.make_async_remote_copy(
            src_ref=spread_out.at[:, peer],
            dst_ref=spread_in.at[:, me],
            send_sem=send_d.at[1],
            recv_sem=recv_d.at[1],
            device_id={"pw": peer},
            device_id_type=MESH,
        ).start()

    pltpu.make_async_copy(spread_out.at[:, me], spread_in.at[:, me], load_sem.at[12]).start()

    landed = row_in.at[pl.ds(0, W - 1)]
    pltpu.make_async_copy(landed, landed, recv_r.at[2]).wait()
    lane = lax.broadcasted_iota(jnp.int32, (1, 128), 1)
    totals = jnp.sum(row_in_rows[...], axis=0, keepdims=True) * (1.0 / float(G**3))
    inter = [
        jnp.sum(jnp.where(lane == k, totals, 0.0), axis=1, keepdims=True) for k in range(8)
    ]

    for n in range(2):
        landed = in_r.at[n, :, pl.ds(0, W - 1)]
        pltpu.make_async_copy(landed, landed, recv_r.at[n]).wait()
        pltpu.make_async_copy(out_r.at[n, :, me], in_r.at[n, :, me], load_sem.at[10 + n]).wait()

        @pl.loop(0, R)
        def _(i):
            parts = tiles_at(in_r_rows, (n * BLOCKS + i * 9) * W)
            app = spin(table_left(il_h[...], il_l[...], parts), -1.0)
            kinetic = kinetic_plane(R * me + i)
            shifted = kinetic - energies[0, n]
            scale = 1.0 / (1.0 + kinetic)
            real = jnp.concatenate((app[0], app[2][:, :64]), axis=1)
            imag = jnp.concatenate((app[1], swap64(app[2])[:, :64]), axis=1)
            resp_real, resp_imag = raw[2 * n + 1, 0, i], raw[2 * n + 1, 1, i]
            real = real + shifted * resp_real
            imag = imag + shifted * resp_imag
            for m in range(2):
                orb_real, orb_imag = raw[2 * m, 0, i], raw[2 * m, 1, i]
                over_real, over_imag = inter[(m * 2 + n) * 2], inter[(m * 2 + n) * 2 + 1]
                real = real - (over_real * orb_real - over_imag * orb_imag)
                imag = imag - (over_imag * orb_real + over_real * orb_imag)
            new_buf[n, 0, i] = resp_real - real * scale
            new_buf[n, 1, i] = resp_imag - imag * scale

        pltpu.make_async_copy(new_buf.at[n], new_hbm.at[0, n], store_sem.at[n]).start()

    landed = spread_in.at[:, pl.ds(0, W - 1)]
    pltpu.make_async_copy(landed, landed, recv_d.at[1]).wait()
    pltpu.make_async_copy(spread_out.at[:, me], spread_in.at[:, me], load_sem.at[12]).wait()
    mirror_rest.wait()

    @pl.when(jnp.logical_not(alone))
    def _():
        mirror_first().wait()

    ends = fold_sum[4] + swap64(fold_mirror[4])
    local = (
        (fold_sum[0] + fold_mirror[0], fold_sum[1] + fold_mirror[1]),
        (fold_sum[2] + fold_mirror[3], ends),
        (fold_sum[3] + fold_mirror[2], swap64(ends)),
    )
    for i in range(R):

        def arrived(t):
            return spread_in_rows[pl.ds((t * R + i) * W, W), :]

        top = jnp.concatenate((arrived(0), arrived(2), arrived(3)), axis=0)
        pair = arrived(4)
        end = jnp.concatenate((arrived(1), pair, swap64(pair)), axis=0)
        total = exact_left(merge[...], jnp.concatenate((top, end), axis=1)) + exact_left(
            expand[...], jnp.concatenate(local[i], axis=1)
        )
        dens_buf[i] = total[:, :G] * 0.125
    dens_out = pltpu.make_async_copy(dens_buf, dens_hbm, store_sem.at[2])
    dens_out.start()

    for u in range(4):
        left = out_a.at[u, :, pl.ds(0, W - 1)]
        pltpu.make_async_copy(left, left, send_a.at[u]).wait()
    for n in range(2):
        left = out_r.at[n, :, pl.ds(0, W - 1)]
        pltpu.make_async_copy(left, left, send_r.at[n]).wait()
    left = row_in.at[pl.ds(0, W - 1)]
    pltpu.make_async_copy(left, left, send_r.at[2]).wait()
    left = spread_out.at[:, pl.ds(0, W - 1)]
    pltpu.make_async_copy(left, left, send_d.at[1]).wait()
    for n in range(2):
        pltpu.make_async_copy(new_buf.at[n], new_hbm.at[0, n], store_sem.at[n]).wait()
    dens_out.wait()


def body(orbitals, responses, energies, weights, potential, perturbation):
    held = [jnp.asarray(table) for table in tables()]
    anywhere = pl.BlockSpec(memory_space=pl.ANY)
    scalar = pl.BlockSpec(memory_space=pltpu.SMEM)
    vmem, dma = pltpu.VMEM, pltpu.SemaphoreType.DMA
    return pl.pallas_call(
        kernel,
        out_shape=(
            jax.ShapeDtypeStruct((1, 2, 2, R, G, G), F32),
            jax.ShapeDtypeStruct((R, G, G), F32),
        ),
        in_specs=[anywhere] * 4 + [scalar] * 2 + [anywhere] * len(held),
        out_specs=(anywhere, anywhere),
        scratch_shapes=[vmem(table.shape, BF16) for table in held]
        + [
            vmem((4, 2, R, G, G), F32),
            vmem((R, G, G), F32),
            vmem((R, G, G), F32),
            vmem((4, BLOCKS, W, 1, 128), F32),
            vmem((4, BLOCKS, W, 1, 128), F32),
            vmem((2, BLOCKS, W, 1, 128), F32),
            vmem((2, BLOCKS, W, 1, 128), F32),
            vmem((R, 3, G, 128), F32),
            vmem((R, 3, G, 128), F32),
            vmem((R, G, 256), F32),
            vmem((5, H, 128), F32),
            vmem((5, H, 128), F32),
            vmem((5, H, 128), F32),
            vmem((5, H, 128), F32),
            vmem((15, W, 1, 128), F32),
            vmem((15, W, 1, 128), F32),
            vmem((8, 8, 128), F32),
            vmem((8, 8, G), F32),
            vmem((1, 128), F32),
            vmem((W, 1, 128), F32),
            vmem((2, 2, R, G, G), F32),
            vmem((R, G, G), F32),
            dma((13,)),
            dma((14,)),
            dma((4,)),
            dma((4,)),
            dma((3,)),
            dma((3,)),
            dma((4,)),
            dma((4,)),
            dma((3,)),
        ],
        compiler_params=pltpu.CompilerParams(
            collective_id=0, has_side_effects=True, vmem_limit_bytes=52 * 2**20
        ),
    )(
        orbitals,
        responses,
        jnp.transpose(potential, (1, 0, 2)),
        jnp.transpose(perturbation, (1, 0, 2)),
        energies,
        weights,
        *held,
    )


def solution(mesh):
    placed = (
        P("pool", None, None, "pw", None, None),
        P("pool", None, None, "pw", None, None),
        P("pool", None),
        P("pool"),
        P(None, "pw", None),
        P(None, "pw", None),
    )
    return jax.shard_map(
        body,
        mesh=mesh,
        in_specs=placed,
        out_specs=(P("pool", None, None, "pw", None, None), P("pw", None, None)),
        check_vma=False,
    )
```

time: 597 us -> 113 us (0.19)
  the two profiles are of different devices: /device:TPU:0 before, /device:TPU:1 now
where the time goes in v1:
time: 113 us; the launch traced here: 112 us
  Pallas kernels  94.5 us (84%)
  local copies, waits for them, and re-layouts  16.4 us (15%)
  between operations  1.32 us (1%)
    pallas_call x1, Pallas kernels, body(): pl.pallas_call(kernel, out_shape=(jax.ShapeDtypeStruct((1, 2, 2, R, G, G)...  94.5 us
    unnamed x32, local copies, waits for them, and re-layouts  16.4 us

profile of v1, /device:TPU:1, one launch (start us, length us, event | category | flops | bytes accessed | tf_op | source)
XLA Modules:
  0.0 112.2 jit_solution(3651674667805427527)
XLA Ops:
  1.3 0.0 copy-start
  1.3 1.0 copy-done
  2.2 0.0 copy-start.1
  2.2 0.9 copy-done.1
  3.2 0.0 copy-start.2
  3.2 0.9 copy-done.2
  4.1 0.0 copy-start.3
  4.1 0.9 copy-done.3
  5.0 0.0 copy-start.4
  5.0 0.9 copy-done.4
  6.0 0.9 copy-done.5
  6.9 0.9 copy-done.6
  7.8 0.9 copy-done.7
  8.7 0.9 copy-done.8
  9.6 0.9 copy-done.9
  10.5 0.8 copy-done.10
  11.3 0.8 copy-done.11
  12.1 0.8 copy-done.12
  12.9 0.7 copy-done.13
  13.6 94.5 %shard_map.203 = (f32[1,2,2,3,192,192]{5,4,3,2,1,0:T(8,128)}, f32[3,192,192]{2,1,0:T(8,128)}) custom-call(f32[1,2,2,3,192,192]{5,4,3,2,1,0:T(8,128)} %orb_hbm.1, f32[1,2,2,3,192,192]{5,4,3,2,1,0:T(8,128)} %resp_hbm.1, f32[3,192,192]{2,1,0:T(8,128)} %bitcast.2, f32[3,192,192]{2,1,0:T(8,128)} %bitcast.3, f32[1,2]{1,0:T(1,128)S(1)} %copy-done.13, ...), custom_call_target="tpu_custom_call" | custom-call | tf_op jit(solution)/shard_map/pallas_call | solution.py:499
  108.1 0.0 copy-start.14
  108.1 3.3 %copy.25 = f32[1,2,2,3,192,192]{5,4,3,2,1,0:T(8,128)} copy(f32[1,2,2,3,192,192]{5,4,3,2,1,0:T(8,128)} %get-tuple-element.4) | data formatting | bytes 3538944
  111.4 0.0 copy-done.14
  111.4 0.8 copy.26
  (9 shorter events, 0.0 us)
Async XLA Ops:
  1.3 1.0 copy-start
  2.2 0.9 copy-start.1
  3.2 0.9 copy-start.2
  4.1 0.9 copy-start.3
  5.0 0.9 copy-start.4
  6.0 0.9 copy-start.5
  6.9 0.9 copy-start.6
  7.8 0.9 copy-start.7
  8.7 0.9 copy-start.8
  9.6 0.9 copy-start.9
  10.5 0.8 copy-start.10
  11.3 0.8 copy-start.11
  12.1 0.8 copy-start.12
  12.9 0.7 copy-start.13
  108.1 3.3 %copy-start.14 = (f32[3,192,192]{2,1,0:T(8,128)S(1)}, f32[3,192,192]{2,1,0:T(8,128)}, u32[]{:S(2)}) copy-start(f32[3,192,192]{2,1,0:T(8,128)} %get-tuple-element.5) | copy-start | bytes 1327108

commit v2 on v1

v2 whole, which is shorter than its diff:
```python
import functools
import math

import jax
import jax.numpy as jnp
import ml_dtypes
import numpy as np
from jax import lax
from jax.experimental import pallas as pl
from jax.experimental.pallas import tpu as pltpu
from jax.sharding import PartitionSpec as P

RECIPROCAL_SQUARE = 0.023428
G = 192
W = 64
R = 3
H = 104
BLOCKS = 27
MESH = pl.DeviceIdType.MESH
F32 = jnp.float32
BF16 = jnp.bfloat16


def halves(table):
    high = table.astype(ml_dtypes.bfloat16)
    low = (table - high.astype(np.float64)).astype(ml_dtypes.bfloat16)
    return [high, low]


def tables():
    index = np.arange(G)
    angles = (np.outer(index, index) % G) * (2.0 * math.pi / G)
    cosine = np.cos(angles) / math.sqrt(G)
    sine = np.sin(angles) / math.sqrt(G)
    spread = np.array([R * (s % W) + s // W for s in range(G)])

    def packed(left, right):
        return np.concatenate(
            (left[:, :128], right[:, :128], left[:, 128:], right[:, 128:]), axis=1
        )

    out_left = np.concatenate((cosine[spread], sine[spread]), axis=0)
    in_left = np.concatenate((cosine[:, spread], sine[:, spread]), axis=0)
    right_real = packed(cosine, sine)
    right_imag = packed(-sine, cosine)
    back_real = packed(cosine, -sine)
    back_imag = packed(sine, cosine)
    back = np.concatenate(
        (back_real[:128], back_imag[:128], back_real[128:], back_imag[128:]), axis=0
    )
    fold = np.zeros((H, G))
    unfold = np.zeros((G, H))
    merge = np.zeros((G, G))
    expand = np.zeros((G, H))
    for a in range(H):
        fold[a, a] += 1.0
        fold[a, -a % G] += 1.0
    for s in range(G):
        a = spread[s]
        unfold[s, min(a, G - a)] = 1.0
        merge[a, s] += 1.0
        merge[-a % G, s] += 1.0
        expand[s, min(s, G - s)] = 1.0
    held = []
    for table in (right_real, right_imag, out_left, in_left, back):
        held += halves(table)
    return held + [m.astype(ml_dtypes.bfloat16) for m in (fold, unfold, merge, expand)]


def split(values):
    high = values.astype(BF16)
    return high, (values - high.astype(F32)).astype(BF16)


def dot(left, right):
    return jnp.dot(left, right, preferred_element_type=F32)


def table_left(high, low, values):
    top, rest = split(values)
    return dot(high, top) + (dot(high, rest) + dot(low, top))


def table_right(values, high, low):
    top, rest = split(values)
    return dot(top, high) + (dot(rest, high) + dot(top, low))


def exact_left(table, values):
    top, rest = split(values)
    last = (values - top.astype(F32) - rest.astype(F32)).astype(BF16)
    return dot(table, top) + (dot(table, rest) + dot(table, last))


def swap64(values):
    return pltpu.roll(values, 64, axis=1)


def lane_sign():
    return jnp.where(lax.broadcasted_iota(jnp.int32, (1, 128), 1) < 64, -1.0, 1.0).astype(F32)


def spin(product, sign):
    cos_part, sin_part = product[:G], product[G:]
    return (
        cos_part[:, :128] - sign * sin_part[:, 128:256],
        cos_part[:, 128:256] + sign * sin_part[:, :128],
        cos_part[:, 256:] + (sign * lane_sign()) * swap64(sin_part[:, 256:]),
    )


def rows_of(start, count):
    if isinstance(start, int):
        return pl.ds(start, count)
    return pl.ds(pl.multiple_of(start, 8), count)


def tiles_at(view, start):
    return jnp.concatenate([view[rows_of(start + t * G, G), :] for t in range(3)], axis=1)


def row_sums(values):
    total = values[0:8]
    for s in range(8, G, 8):
        total = total + values[s : s + 8]
    return total


def squared_freq(index):
    freq = jnp.where(index < G // 2, index, index - G).astype(F32)
    return freq * freq


def kinetic_plane(row):
    plane = squared_freq(lax.broadcasted_iota(jnp.int32, (G, G), 0))
    plane = plane + squared_freq(lax.broadcasted_iota(jnp.int32, (G, G), 1))
    return (0.5 * RECIPROCAL_SQUARE) * (squared_freq(row) + plane)


def kernel(
    orb_hbm, resp_hbm, pot_hbm, pert_hbm, energies, weights, *refs
):
    table_hbm = refs[:14]
    new_out, dens_out = refs[14:16]
    tables_in = refs[16:30]
    (
        raw, pot, pert, out_a, in_a, out_r, in_r, orb_space, app_space, dens,
        fold_mine, fold_other, fold_sum, fold_mirror, spread_out, spread_in,
        sums, sums_g, row_out, row_in,
        load_sem, table_sem, send_a, recv_a, send_r, recv_r, send_d, recv_d,
    ) = refs[30:]
    (wr_h, wr_l, wi_h, wi_l, ol_h, ol_l, il_h, il_l, bk_h, bk_l, fold, unfold, merge, expand) = tables_in

    me = lax.axis_index("pw")
    pool = lax.axis_index("pool")

    def load_table(k):
        return pltpu.make_async_copy(table_hbm[k], tables_in[k], table_sem.at[k])

    def load_unit(u):
        source = orb_hbm if u % 2 == 0 else resp_hbm
        return pltpu.make_async_copy(source.at[0, u // 2], raw.at[u], load_sem.at[u])

    loads_pot = pltpu.make_async_copy(pot_hbm, pot, load_sem.at[4])
    loads_pert = pltpu.make_async_copy(pert_hbm, pert, load_sem.at[5])
    for k in range(4):
        load_table(k).start()
    load_unit(0).start()
    for k in range(4, 6):
        load_table(k).start()
    for u in range(1, 4):
        load_unit(u).start()
    for k in range(6, 14):
        load_table(k).start()
    loads_pot.start()
    loads_pert.start()

    barrier = pltpu.get_barrier_semaphore()

    def peer_at(k):
        return me ^ (1 + (k * 37 + 11) % (W - 1))

    @pl.loop(0, W - 1, unroll=9)
    def _(k):
        pl.semaphore_signal(barrier, inc=1, device_id={"pw": peer_at(k)}, device_id_type=MESH)

    pl.semaphore_signal(barrier, inc=1, device_id={"pool": 1 - pool}, device_id_type=MESH)

    out_a_rows = out_a.reshape(4 * BLOCKS * W, 128)
    in_a_rows = in_a.reshape(4 * BLOCKS * W, 128)
    out_r_rows = out_r.reshape(2 * BLOCKS * W, 128)
    in_r_rows = in_r.reshape(2 * BLOCKS * W, 128)
    spread_out_rows = spread_out.reshape(15 * W, 128)
    spread_in_rows = spread_in.reshape(15 * W, 128)
    row_in_rows = row_in.reshape(W, 128)

    for k in range(6):
        load_table(k).wait()

    def piece_a(ref, u, part, who):
        if u == 0:
            return ref.at[u, :, part, who]
        if u == 1:
            return ref.at[u, :, :, who]
        return ref.at[u, pl.ds(3 * part, 3), :, who]

    def send_piece_a(u, part, peer):
        pltpu.make_async_remote_copy(
            src_ref=piece_a(out_a, u, part, peer),
            dst_ref=piece_a(in_a, u, part, me),
            send_sem=send_a.at[u, part],
            recv_sem=recv_a.at[u, part],
            device_id={"pw": peer},
            device_id_type=MESH,
        ).start()

    def wait_bytes(ref, sem):
        pltpu.make_async_copy(ref, ref, sem).wait()

    others = pl.ds(0, W - 1)

    def own_a(u):
        return pltpu.make_async_copy(
            out_a.at[u, :, :, me], in_a.at[u, :, :, me], load_sem.at[6 + u]
        )

    def plane(u, i):
        planes = table_right(raw[u, 0, i], wr_h[...], wr_l[...]) + table_right(
            raw[u, 1, i], wi_h[...], wi_l[...]
        )
        parts = spin(table_left(ol_h[...], ol_l[...], planes), 1.0)
        for j in range(R):
            for t in range(3):
                start = (u * BLOCKS + (j * 3 + t) * R + i) * W
                out_a_rows[rows_of(start, W), :] = parts[t][j * W : (j + 1) * W]

    load_unit(0).wait()
    for i in range(R):
        plane(0, i)
        if i == 0:
            pl.semaphore_wait(barrier, W)

        @pl.loop(0, W - 1, unroll=9)
        def _(k):
            send_piece_a(0, i, peer_at(k))

    own_a(0).start()
    for u in range(1, 4):
        load_unit(u).wait()

        @pl.loop(0, R)
        def _(i):
            plane(u, i)

        if u == 1:

            @pl.loop(0, W - 1, unroll=9)
            def _(k):
                send_piece_a(1, 0, peer_at(k))

        own_a(u).start()

    for j in range(R):

        @pl.loop(0, W - 1, unroll=9)
        def _(k):
            peer = peer_at(k)
            send_piece_a(2, j, peer)
            send_piece_a(3, j, peer)

    for k in range(6, 14):
        load_table(k).wait()

    sums_g[...] = jnp.zeros_like(sums_g)

    @pl.loop(0, R)
    def _(i):
        kinetic = kinetic_plane(R * me + i)
        for n in range(2):
            shifted = kinetic - energies[0, n]
            real = shifted * raw[2 * n + 1, 0, i]
            imag = shifted * raw[2 * n + 1, 1, i]
            for m in range(2):
                left_real, left_imag = raw[2 * m, 0, i], raw[2 * m, 1, i]
                at = (m * 2 + n) * 2
                sums_g[at] += row_sums(left_real * real + left_imag * imag)
                sums_g[at + 1] += row_sums(left_real * imag - left_imag * real)

    loads_pot.wait()
    loads_pert.wait()
    sums[...] = jnp.zeros_like(sums)

    def columns(n, j):
        at = j * 3 * G
        first = 2 * n * BLOCKS * W
        second = (2 * n + 1) * BLOCKS * W
        orb = spin(table_left(il_h[...], il_l[...], tiles_at(in_a_rows, first + at)), 1.0)
        resp = spin(table_left(il_h[...], il_l[...], tiles_at(in_a_rows, second + at)), 1.0)
        pot_top = pot[j, :, 0:128]
        pert_top = pert[j, :, 0:128]
        pot_end = jnp.concatenate((pot[j, :, 128:G], pot[j, :, 128:G]), axis=1)
        pert_end = jnp.concatenate((pert[j, :, 128:G], pert[j, :, 128:G]), axis=1)
        app = (
            pot_top * resp[0] + pert_top * orb[0],
            pot_top * resp[1] + pert_top * orb[1],
            pot_end * resp[2] + pert_end * orb[2],
        )
        ends = orb[2] * resp[2]
        density = (2.0 * weights[0]) * jnp.concatenate(
            (orb[0] * resp[0] + orb[1] * resp[1], ends + swap64(ends)), axis=1
        )

        def overlap(left, right, slot):
            sums[slot] += row_sums(left[0] * right[0] + left[1] * right[1] + left[2] * right[2])
            sums[slot + 1] += row_sums(
                left[0] * right[1]
                - left[1] * right[0]
                - lane_sign() * left[2] * swap64(right[2])
            )

        if n == 0:
            overlap(orb, app, 0)
            dens[j] = density
            for t in range(3):
                orb_space[j, t] = orb[t]
                app_space[j, t] = app[t]
        else:
            dens[j] = dens[j] + density
            orb_first = [orb_space[j, t] for t in range(3)]
            app_first = [app_space[j, t] for t in range(3)]
            overlap(orb_first, app, 2)
            overlap(orb, app_first, 4)
            overlap(orb, app, 6)
        product = table_left(ol_h[...], ol_l[...], jnp.concatenate(app, axis=1))
        turned = jnp.concatenate(spin(product, -1.0), axis=1)
        back = table_right(turned, bk_h[...], bk_l[...])
        for i in range(R):
            for t in range(3):
                start = (n * BLOCKS + (i * 3 + t) * R + j) * W
                out_r_rows[rows_of(start, W), :] = back[
                    i * W : (i + 1) * W, t * 128 : (t + 1) * 128
                ]

    def piece_r(ref, n, part, who):
        if n == 0:
            return ref.at[n, :, :, who]
        return ref.at[n, :, part, who]

    def send_piece_r(n, part, peer):
        pltpu.make_async_remote_copy(
            src_ref=piece_r(out_r, n, part, peer),
            dst_ref=piece_r(in_r, n, part, me),
            send_sem=send_r.at[n, part],
            recv_sem=recv_r.at[n, part],
            device_id={"pw": peer},
            device_id_type=MESH,
        ).start()

    def own_r(n):
        return pltpu.make_async_copy(
            out_r.at[n, :, :, me], in_r.at[n, :, :, me], load_sem.at[10 + n]
        )

    for i in range(R):
        wait_bytes(piece_a(in_a, 0, i, others), recv_a.at[0, i])
    wait_bytes(piece_a(in_a, 1, 0, others), recv_a.at[1, 0])
    own_a(0).wait()
    own_a(1).wait()

    @pl.loop(0, R)
    def _(j):
        columns(0, j)

    @pl.loop(0, W - 1, unroll=9)
    def _(k):
        send_piece_r(0, 0, peer_at(k))

    own_r(0).start()
    own_a(2).wait()
    own_a(3).wait()

    strips_of = ((0, 2), (2, 1), (3, 2))

    def pool_copy(j):
        strips = pl.ds(*strips_of[j])
        return pltpu.make_async_remote_copy(
            src_ref=fold_mine.at[strips],
            dst_ref=fold_other.at[strips],
            send_sem=send_d.at[j],
            recv_sem=recv_d.at[j],
            device_id={"pool": 1 - pool},
            device_id_type=MESH,
        )

    lane = lax.broadcasted_iota(jnp.int32, (1, 128), 1)
    for j in range(R):
        for u in (2, 3):
            wait_bytes(piece_a(in_a, u, j, others), recv_a.at[u, j])
        columns(1, j)
        if j == 0:
            strips = (dens[0, :, 0:128], dens[0, :, 128:256])
        elif j == 1:
            strips = (dens[1, :, 0:128],)
        else:
            strips = (
                dens[2, :, 0:128],
                jnp.where(lane < 64, dens[1, :, 128:256], dens[2, :, 128:256]),
            )
        first, count = strips_of[j]
        folded = exact_left(fold[...], jnp.concatenate(strips, axis=1))
        for t in range(count):
            fold_mine[first + t] = folded[:, t * 128 : (t + 1) * 128]
        pool_copy(j).start()

        @pl.loop(0, W - 1, unroll=9)
        def _(k):
            send_piece_r(1, j, peer_at(k))

    own_r(1).start()
    row = jnp.zeros((1, 128), F32)
    for k in range(8):
        one = jnp.sum(sums[k], keepdims=True) + jnp.sum(sums_g[k], keepdims=True)
        row = jnp.where(lane == k, one, row)
    row_out[...] = row
    row_in[me] = row

    @pl.loop(0, W - 1, unroll=9)
    def _(k):
        pltpu.make_async_remote_copy(
            src_ref=row_out,
            dst_ref=row_in.at[me],
            send_sem=send_r.at[2, 0],
            recv_sem=recv_r.at[2, 0],
            device_id={"pw": peer_at(k)},
            device_id_type=MESH,
        ).start()

    for j in range(R):
        pool_copy(j).wait()
    for t in range(5):
        fold_sum[t] = fold_mine[t] + fold_other[t]
    whole = exact_left(unfold[...], jnp.concatenate([fold_sum[t] for t in range(5)], axis=1))
    for t in range(5):
        spread_out_rows[pl.ds(t * G, G), :] = whole[:, t * 128 : (t + 1) * 128]

    opposite = (W - me) % W
    alone = opposite == me

    def mirror_first():
        return pltpu.make_async_remote_copy(
            src_ref=fold_sum.at[pl.ds(0, 2)],
            dst_ref=fold_mirror.at[pl.ds(0, 2)],
            send_sem=send_d.at[3],
            recv_sem=recv_d.at[3],
            device_id={"pw": opposite},
            device_id_type=MESH,
        )

    mirror_rest = pltpu.make_async_remote_copy(
        src_ref=fold_sum.at[pl.ds(2, 3)],
        dst_ref=fold_mirror.at[pl.ds(2, 3)],
        send_sem=send_d.at[4],
        recv_sem=recv_d.at[4],
        device_id={"pw": W - 1 - me},
        device_id_type=MESH,
    )
    mirror_rest.start()

    @pl.when(jnp.logical_not(alone))
    def _():
        mirror_first().start()

    @pl.when(alone)
    def _():
        for t in range(2):
            fold_mirror[t] = fold_sum[t]

    @pl.loop(0, W - 1, unroll=9)
    def _(k):
        peer = peer_at(k)
        pltpu.make_async_remote_copy(
            src_ref=spread_out.at[:, peer],
            dst_ref=spread_in.at[:, me],
            send_sem=send_d.at[5],
            recv_sem=recv_d.at[5],
            device_id={"pw": peer},
            device_id_type=MESH,
        ).start()

    pltpu.make_async_copy(spread_out.at[:, me], spread_in.at[:, me], load_sem.at[12]).start()

    wait_bytes(row_in.at[others], recv_r.at[2, 0])
    totals = jnp.sum(row_in_rows[...], axis=0, keepdims=True) * (1.0 / float(G**3))
    inter = [
        jnp.sum(jnp.where(lane == k, totals, 0.0), axis=1, keepdims=True) for k in range(8)
    ]

    def update(n):
        @pl.loop(0, R)
        def _(i):
            parts = tiles_at(in_r_rows, (n * BLOCKS + i * 9) * W)
            app = spin(table_left(il_h[...], il_l[...], parts), -1.0)
            kinetic = kinetic_plane(R * me + i)
            shifted = kinetic - energies[0, n]
            scale = 1.0 / (1.0 + kinetic)
            real = jnp.concatenate((app[0], app[2][:, :64]), axis=1)
            imag = jnp.concatenate((app[1], swap64(app[2])[:, :64]), axis=1)
            resp_real, resp_imag = raw[2 * n + 1, 0, i], raw[2 * n + 1, 1, i]
            real = real + shifted * resp_real
            imag = imag + shifted * resp_imag
            for m in range(2):
                orb_real, orb_imag = raw[2 * m, 0, i], raw[2 * m, 1, i]
                over_real, over_imag = inter[(m * 2 + n) * 2], inter[(m * 2 + n) * 2 + 1]
                real = real - (over_real * orb_real - over_imag * orb_imag)
                imag = imag - (over_imag * orb_real + over_real * orb_imag)
            new_out[0, n, 0, i] = resp_real - real * scale
            new_out[0, n, 1, i] = resp_imag - imag * scale


    wait_bytes(piece_r(in_r, 0, 0, others), recv_r.at[0, 0])
    own_r(0).wait()
    update(0)

    wait_bytes(spread_in.at[:, others], recv_d.at[5])
    pltpu.make_async_copy(spread_out.at[:, me], spread_in.at[:, me], load_sem.at[12]).wait()
    mirror_rest.wait()

    @pl.when(jnp.logical_not(alone))
    def _():
        mirror_first().wait()

    ends = fold_sum[4] + swap64(fold_mirror[4])
    local = (
        (fold_sum[0] + fold_mirror[0], fold_sum[1] + fold_mirror[1]),
        (fold_sum[2] + fold_mirror[3], ends),
        (fold_sum[3] + fold_mirror[2], swap64(ends)),
    )
    for i in range(R):

        def arrived(t):
            return spread_in_rows[pl.ds((t * R + i) * W, W), :]

        top = jnp.concatenate((arrived(0), arrived(2), arrived(3)), axis=0)
        pair = arrived(4)
        end = jnp.concatenate((arrived(1), pair, swap64(pair)), axis=0)
        total = exact_left(merge[...], jnp.concatenate((top, end), axis=1)) + exact_left(
            expand[...], jnp.concatenate(local[i], axis=1)
        )
        dens_out[i] = total[:, :G] * 0.125

    for j in range(R):
        wait_bytes(piece_r(in_r, 1, j, others), recv_r.at[1, j])
    own_r(1).wait()
    update(1)

    for j in range(R):
        for u in (0, 2, 3):
            wait_bytes(piece_a(out_a, u, j, others), send_a.at[u, j])
        wait_bytes(piece_r(out_r, 1, j, others), send_r.at[1, j])
    wait_bytes(piece_a(out_a, 1, 0, others), send_a.at[1, 0])
    wait_bytes(piece_r(out_r, 0, 0, others), send_r.at[0, 0])
    wait_bytes(row_in.at[others], send_r.at[2, 0])
    wait_bytes(spread_out.at[:, others], send_d.at[5])


def in_hbm(array):
    return pltpu.with_memory_space_constraint(array, pltpu.HBM)


def body(orbitals, responses, energies, weights, potential, perturbation):
    held = [in_hbm(jnp.asarray(table)) for table in tables()]
    anywhere = pl.BlockSpec(memory_space=pl.ANY)
    scalar = pl.BlockSpec(memory_space=pltpu.SMEM)
    vmem, dma = pltpu.VMEM, pltpu.SemaphoreType.DMA
    return pl.pallas_call(
        kernel,
        out_shape=(
            pltpu.VMEM((1, 2, 2, R, G, G), F32),
            pltpu.VMEM((R, G, G), F32),
        ),
        in_specs=[anywhere] * 4 + [scalar] * 2 + [anywhere] * len(held),
        out_specs=(pl.BlockSpec(memory_space=pltpu.VMEM),) * 2,
        scratch_shapes=[vmem(table.shape, BF16) for table in held]
        + [
            vmem((4, 2, R, G, G), F32),
            vmem((R, G, G), F32),
            vmem((R, G, G), F32),
            vmem((4, 9, R, W, 1, 128), F32),
            vmem((4, 9, R, W, 1, 128), F32),
            vmem((2, 9, R, W, 1, 128), F32),
            vmem((2, 9, R, W, 1, 128), F32),
            vmem((R, 3, G, 128), F32),
            vmem((R, 3, G, 128), F32),
            vmem((R, G, 256), F32),
            vmem((5, H, 128), F32),
            vmem((5, H, 128), F32),
            vmem((5, H, 128), F32),
            vmem((5, H, 128), F32),
            vmem((15, W, 1, 128), F32),
            vmem((15, W, 1, 128), F32),
            vmem((8, 8, 128), F32),
            vmem((8, 8, G), F32),
            vmem((1, 128), F32),
            vmem((W, 1, 128), F32),
            dma((13,)),
            dma((14,)),
            dma((4, R)),
            dma((4, R)),
            dma((3, R)),
            dma((3, R)),
            dma((6,)),
            dma((6,)),
        ],
        compiler_params=pltpu.CompilerParams(
            collective_id=0, has_side_effects=True, vmem_limit_bytes=56 * 2**20
        ),
    )(
        in_hbm(orbitals),
        in_hbm(responses),
        in_hbm(jnp.transpose(potential, (1, 0, 2))),
        in_hbm(jnp.transpose(perturbation, (1, 0, 2))),
        energies,
        weights,
        *held,
    )


def solution(mesh):
    placed = (
        P("pool", None, None, "pw", None, None),
        P("pool", None, None, "pw", None, None),
        P("pool", None),
        P("pool"),
        P(None, "pw", None),
        P(None, "pw", None),
    )
    return jax.shard_map(
        body,
        mesh=mesh,
        in_specs=placed,
        out_specs=(P("pool", None, None, "pw", None, None), P("pw", None, None)),
        check_vma=False,
    )
```

time: 113 us -> 95.6 us (0.85)
  local copies, waits for them, and re-layouts: 16.4 us -> 2.22 us
  Pallas kernels: 94.5 us -> 92 us
    unnamed x32 -> x2, local copies, waits for them, and re-layouts: 16.4 us -> 2.22 us
    pallas_call x1, Pallas kernels: 94.5 us -> 92 us  [body(): pl.pallas_call(kernel, out_shape=(pltpu.VMEM((1, 2, 2, R, G, G), F32), pl...]
where the time goes in v2:
time: 95.6 us; the launch traced here: 95.5 us
  Pallas kernels  92 us (96%)
  local copies, waits for them, and re-layouts  2.22 us (2%)
  between operations  1.29 us (1%)
    pallas_call x1, Pallas kernels, body(): pl.pallas_call(kernel, out_shape=(pltpu.VMEM((1, 2, 2, R, G, G), F32), pl...  92 us
    unnamed x2, local copies, waits for them, and re-layouts  2.22 us

profile of v2, /device:TPU:1, one launch (start us, length us, event | category | flops | bytes accessed | tf_op | source)
XLA Modules:
  0.0 95.5 jit_solution(262095349227729574)
XLA Ops:
  1.3 92.0 %shard_map.203 = (f32[1,2,2,3,192,192]{5,4,3,2,1,0:T(8,128)S(1)}, f32[3,192,192]{2,1,0:T(8,128)S(1)}) custom-call(f32[1,2,2,3,192,192]{5,4,3,2,1,0:T(8,128)} %orb_hbm.1, f32[1,2,2,3,192,192]{5,4,3,2,1,0:T(8,128)} %resp_hbm.1, f32[3,192,192]{2,1,0:T(8,128)} %bitcast.2, f32[3,192,192]{2,1,0:T(8,128)} %bitcast.3, f32[1,2]{1,0:T(1,128)} %energies.1, ...), custom_call_target="tpu_custom_call" | custom-call | tf_op jit(solution)/shard_map/pallas_call | solution.py:575
  93.3 1.4 %copy.24 = f32[1,2,2,3,192,192]{5,4,3,2,1,0:T(8,128)} copy(f32[1,2,2,3,192,192]{5,4,3,2,1,0:T(8,128)S(1)} %get-tuple-element.2) | data formatting | bytes 3538944
  94.7 0.8 copy.25

commit v3 on v2

--- a/solution.py
+++ b/solution.py
@@ -15,6 +15,7 @@
 W = 64
 R = 3
 H = 104
+K = G // 2 + 1
 BLOCKS = 27
 MESH = pl.DeviceIdType.MESH
 F32 = jnp.float32
@@ -168,24 +169,6 @@
     load_unit(0).start()
     for k in range(4, 6):
         load_table(k).start()
-    for u in range(1, 4):
-        load_unit(u).start()
-    for k in range(6, 14):
-        load_table(k).start()
-    loads_pot.start()
-    loads_pert.start()
-
-    barrier = pltpu.get_barrier_semaphore()
-
-    def peer_at(k):
-        return me ^ (1 + (k * 37 + 11) % (W - 1))
-
-    @pl.loop(0, W - 1, unroll=9)
-    def _(k):
-        pl.semaphore_signal(barrier, inc=1, device_id={"pw": peer_at(k)}, device_id_type=MESH)
-
-    pl.semaphore_signal(barrier, inc=1, device_id={"pool": 1 - pool}, device_id_type=MESH)
-
     out_a_rows = out_a.reshape(4 * BLOCKS * W, 128)
     in_a_rows = in_a.reshape(4 * BLOCKS * W, 128)
     out_r_rows = out_r.reshape(2 * BLOCKS * W, 128)
@@ -193,6 +176,37 @@
     spread_out_rows = spread_out.reshape(15 * W, 128)
     spread_in_rows = spread_in.reshape(15 * W, 128)
     row_in_rows = row_in.reshape(W, 128)
+    fold_mine_rows = fold_mine.reshape(5 * H, 128)
+    fold_other_rows = fold_other.reshape(5 * H, 128)
+    fold_sum_rows = fold_sum.reshape(5 * H, 128)
+    fold_mirror_rows = fold_mirror.reshape(5 * H, 128)
+
+    for t in range(5):
+        fold_other_rows[pl.ds(t * H + H - 8, 8), :] = jnp.zeros((8, 128), F32)
+        fold_mirror_rows[pl.ds(t * H + H - 8, 8), :] = jnp.zeros((8, 128), F32)
+    kept = pl.ds(0, K)
+    mirrors = ((W - me) % W, W - 1 - me)
+
+    barrier = pltpu.get_barrier_semaphore()
+
+    def peer_at(k):
+        return me ^ (1 + (k * 37 + 11) % (W - 1))
+
+    @pl.loop(0, W - 1, unroll=9)
+    def _(k):
+        pl.semaphore_signal(barrier, inc=1, device_id={"pw": peer_at(k)}, device_id_type=MESH)
+
+    for who in (me, *mirrors):
+        pl.semaphore_signal(
+            barrier, inc=1, device_id={"pool": 1 - pool, "pw": who}, device_id_type=MESH
+        )
+
+    for u in range(1, 4):
+        load_unit(u).start()
+    for k in range(6, 14):
+        load_table(k).start()
+    loads_pot.start()
+    loads_pert.start()
 
     for k in range(6):
         load_table(k).wait()
@@ -238,7 +252,7 @@
     for i in range(R):
         plane(0, i)
         if i == 0:
-            pl.semaphore_wait(barrier, W)
+            pl.semaphore_wait(barrier, W + 2)
 
         @pl.loop(0, W - 1, unroll=9)
         def _(k):
@@ -384,8 +398,8 @@
     def pool_copy(j):
         strips = pl.ds(*strips_of[j])
         return pltpu.make_async_remote_copy(
-            src_ref=fold_mine.at[strips],
-            dst_ref=fold_other.at[strips],
+            src_ref=fold_mine.at[strips, kept],
+            dst_ref=fold_other.at[strips, kept],
             send_sem=send_d.at[j],
             recv_sem=recv_d.at[j],
             device_id={"pool": 1 - pool},
@@ -409,7 +423,7 @@
         first, count = strips_of[j]
         folded = exact_left(fold[...], jnp.concatenate(strips, axis=1))
         for t in range(count):
-            fold_mine[first + t] = folded[:, t * 128 : (t + 1) * 128]
+            fold_mine_rows[pl.ds((first + t) * H, H), :] = folded[:, t * 128 : (t + 1) * 128]
         pool_copy(j).start()
 
         @pl.loop(0, W - 1, unroll=9)
@@ -437,43 +451,28 @@
 
     for j in range(R):
         pool_copy(j).wait()
+    summed = [
+        fold_mine_rows[pl.ds(t * H, H), :] + fold_other_rows[pl.ds(t * H, H), :] for t in range(5)
+    ]
     for t in range(5):
-        fold_sum[t] = fold_mine[t] + fold_other[t]
-    whole = exact_left(unfold[...], jnp.concatenate([fold_sum[t] for t in range(5)], axis=1))
+        fold_sum_rows[pl.ds(t * H, H), :] = summed[t]
+    whole = exact_left(unfold[...], jnp.concatenate(summed, axis=1))
     for t in range(5):
         spread_out_rows[pl.ds(t * G, G), :] = whole[:, t * 128 : (t + 1) * 128]
 
-    opposite = (W - me) % W
-    alone = opposite == me
-
-    def mirror_first():
+    def mirror_copy(part):
+        strips = (pl.ds(0, 2), pl.ds(2, 3))[part]
         return pltpu.make_async_remote_copy(
-            src_ref=fold_sum.at[pl.ds(0, 2)],
-            dst_ref=fold_mirror.at[pl.ds(0, 2)],
-            send_sem=send_d.at[3],
-            recv_sem=recv_d.at[3],
-            device_id={"pw": opposite},
+            src_ref=fold_sum.at[strips, kept],
+            dst_ref=fold_mirror.at[strips, kept],
+            send_sem=send_d.at[3 + part],
+            recv_sem=recv_d.at[3 + part],
+            device_id={"pool": 1 - pool, "pw": mirrors[part]},
             device_id_type=MESH,
         )
 
-    mirror_rest = pltpu.make_async_remote_copy(
-        src_ref=fold_sum.at[pl.ds(2, 3)],
-        dst_ref=fold_mirror.at[pl.ds(2, 3)],
-        send_sem=send_d.at[4],
-        recv_sem=recv_d.at[4],
-        device_id={"pw": W - 1 - me},
-        device_id_type=MESH,
-    )
-    mirror_rest.start()
-
-    @pl.when(jnp.logical_not(alone))
-    def _():
-        mirror_first().start()
-
-    @pl.when(alone)
-    def _():
-        for t in range(2):
-            fold_mirror[t] = fold_sum[t]
+    for part in range(2):
+        mirror_copy(part).start()
 
     @pl.loop(0, W - 1, unroll=9)
     def _(k):
@@ -521,19 +520,22 @@
     own_r(0).wait()
     update(0)
 
+    for j in range(R):
+        wait_bytes(piece_r(in_r, 1, j, others), recv_r.at[1, j])
+    own_r(1).wait()
+    update(1)
+
     wait_bytes(spread_in.at[:, others], recv_d.at[5])
     pltpu.make_async_copy(spread_out.at[:, me], spread_in.at[:, me], load_sem.at[12]).wait()
-    mirror_rest.wait()
-
-    @pl.when(jnp.logical_not(alone))
-    def _():
-        mirror_first().wait()
-
-    ends = fold_sum[4] + swap64(fold_mirror[4])
+    for part in range(2):
+        mirror_copy(part).wait()
+    own = [fold_sum_rows[pl.ds(t * H, H), :] for t in range(5)]
+    seen = [fold_mirror_rows[pl.ds(t * H, H), :] for t in range(5)]
+    ends = own[4] + swap64(seen[4])
     local = (
-        (fold_sum[0] + fold_mirror[0], fold_sum[1] + fold_mirror[1]),
-        (fold_sum[2] + fold_mirror[3], ends),
-        (fold_sum[3] + fold_mirror[2], swap64(ends)),
+        (own[0] + seen[0], own[1] + seen[1]),
+        (own[2] + seen[3], ends),
+        (own[3] + seen[2], swap64(ends)),
     )
     for i in range(R):
 
@@ -547,11 +549,6 @@
             expand[...], jnp.concatenate(local[i], axis=1)
         )
         dens_out[i] = total[:, :G] * 0.125
-
-    for j in range(R):
-        wait_bytes(piece_r(in_r, 1, j, others), recv_r.at[1, j])
-    own_r(1).wait()
-    update(1)
 
     for j in range(R):
         for u in (0, 2, 3):
@@ -592,10 +589,10 @@
             vmem((R, 3, G, 128), F32),
             vmem((R, 3, G, 128), F32),
             vmem((R, G, 256), F32),
-            vmem((5, H, 128), F32),
-            vmem((5, H, 128), F32),
-            vmem((5, H, 128), F32),
-            vmem((5, H, 128), F32),
+            vmem((5, H, 1, 128), F32),
+            vmem((5, H, 1, 128), F32),
+            vmem((5, H, 1, 128), F32),
+            vmem((5, H, 1, 128), F32),
             vmem((15, W, 1, 128), F32),
             vmem((15, W, 1, 128), F32),
             vmem((8, 8, 128), F32),

time: 95.6 us -> 92.2 us (0.964)
  Pallas kernels: 92 us -> 88.6 us
    pallas_call x1, Pallas kernels: 92 us -> 88.6 us  [body(): pl.pallas_call(kernel, out_shape=(pltpu.VMEM((1, 2, 2, R, G, G), F32), pl...]
where the time goes in v3:
time: 92.2 us; the launch traced here: 92.1 us
  Pallas kernels  88.6 us (96%)
  local copies, waits for them, and re-layouts  2.22 us (2%)
  between operations  1.29 us (1%)
    pallas_call x1, Pallas kernels, body(): pl.pallas_call(kernel, out_shape=(pltpu.VMEM((1, 2, 2, R, G, G), F32), pl...  88.6 us
    unnamed x2, local copies, waits for them, and re-layouts  2.22 us

profile of v3, /device:TPU:1, one launch (start us, length us, event | category | flops | bytes accessed | tf_op | source)
XLA Modules:
  0.0 92.1 jit_solution(3502063053510966565)
XLA Ops:
  1.3 88.6 %shard_map.203 = (f32[1,2,2,3,192,192]{5,4,3,2,1,0:T(8,128)S(1)}, f32[3,192,192]{2,1,0:T(8,128)S(1)}) custom-call(f32[1,2,2,3,192,192]{5,4,3,2,1,0:T(8,128)} %orb_hbm.1, f32[1,2,2,3,192,192]{5,4,3,2,1,0:T(8,128)} %resp_hbm.1, f32[3,192,192]{2,1,0:T(8,128)} %bitcast.2, f32[3,192,192]{2,1,0:T(8,128)} %bitcast.3, f32[1,2]{1,0:T(1,128)} %energies.1, ...), custom_call_target="tpu_custom_call" | custom-call | tf_op jit(solution)/shard_map/pallas_call | solution.py:572
  89.9 1.4 %copy.24 = f32[1,2,2,3,192,192]{5,4,3,2,1,0:T(8,128)} copy(f32[1,2,2,3,192,192]{5,4,3,2,1,0:T(8,128)S(1)} %get-tuple-element.2) | data formatting | bytes 3538944
  91.3 0.8 copy.25

commit v4 on v3

--- a/solution.py
+++ b/solution.py
@@ -15,7 +15,8 @@
 W = 64
 R = 3
 H = 104
-K = G // 2 + 1
+C = 14
+K = 7 * C
 BLOCKS = 27
 MESH = pl.DeviceIdType.MESH
 F32 = jnp.float32
@@ -395,16 +396,58 @@
 
     strips_of = ((0, 2), (2, 1), (3, 2))
 
-    def pool_copy(j):
+    def pool_copy(j, rows):
         strips = pl.ds(*strips_of[j])
         return pltpu.make_async_remote_copy(
-            src_ref=fold_mine.at[strips, kept],
-            dst_ref=fold_other.at[strips, kept],
+            src_ref=fold_mine.at[strips, rows],
+            dst_ref=fold_other.at[strips, rows],
             send_sem=send_d.at[j],
             recv_sem=recv_d.at[j],
             device_id={"pool": 1 - pool},
             device_id_type=MESH,
         )
+
+    def mirror_copy(j, rows):
+        strips = pl.ds(*strips_of[j])
+        return pltpu.make_async_remote_copy(
+            src_ref=fold_sum.at[strips, rows],
+            dst_ref=fold_mirror.at[strips, rows],
+            send_sem=send_d.at[3 + j],
+            recv_sem=recv_d.at[3 + j],
+            device_id={"pool": 1 - pool, "pw": mirrors[min(j, 1)]},
+            device_id_type=MESH,
+        )
+
+    def piece_d(ref, j, who):
+        first, count = strips_of[j]
+        return ref.at[pl.ds(3 * first, 3 * count), who]
+
+    def spread(j):
+        first, count = strips_of[j]
+        pool_copy(j, kept).wait()
+        summed = [
+            fold_mine_rows[pl.ds(t * H, H), :] + fold_other_rows[pl.ds(t * H, H), :]
+            for t in range(first, first + count)
+        ]
+        for t in range(count):
+            fold_sum_rows[pl.ds((first + t) * H, H), :] = summed[t]
+        whole = exact_left(unfold[...], jnp.concatenate(summed, axis=1))
+        for t in range(count):
+            spread_out_rows[pl.ds((first + t) * G, G), :] = whole[:, t * 128 : (t + 1) * 128]
+
+        @pl.loop(0, 7)
+        def _(c):
+            mirror_copy(j, pl.ds(c * C, C)).start()
+            for k in range(9):
+                peer = peer_at(c * 9 + k)
+                pltpu.make_async_remote_copy(
+                    src_ref=piece_d(spread_out, j, peer),
+                    dst_ref=piece_d(spread_in, j, me),
+                    send_sem=send_d.at[6 + j],
+                    recv_sem=recv_d.at[6 + j],
+                    device_id={"pw": peer},
+                    device_id_type=MESH,
+                ).start()
 
     lane = lax.broadcasted_iota(jnp.int32, (1, 128), 1)
     for j in range(R):
@@ -424,11 +467,15 @@
         folded = exact_left(fold[...], jnp.concatenate(strips, axis=1))
         for t in range(count):
             fold_mine_rows[pl.ds((first + t) * H, H), :] = folded[:, t * 128 : (t + 1) * 128]
-        pool_copy(j).start()
-
-        @pl.loop(0, W - 1, unroll=9)
-        def _(k):
-            send_piece_r(1, j, peer_at(k))
+
+        @pl.loop(0, 7)
+        def _(c):
+            pool_copy(j, pl.ds(c * C, C)).start()
+            for k in range(9):
+                send_piece_r(1, j, peer_at(c * 9 + k))
+
+        if j > 0:
+            spread(j - 1)
 
     own_r(1).start()
     row = jnp.zeros((1, 128), F32)
@@ -449,43 +496,7 @@
             device_id_type=MESH,
         ).start()
 
-    for j in range(R):
-        pool_copy(j).wait()
-    summed = [
-        fold_mine_rows[pl.ds(t * H, H), :] + fold_other_rows[pl.ds(t * H, H), :] for t in range(5)
-    ]
-    for t in range(5):
-        fold_sum_rows[pl.ds(t * H, H), :] = summed[t]
-    whole = exact_left(unfold[...], jnp.concatenate(summed, axis=1))
-    for t in range(5):
-        spread_out_rows[pl.ds(t * G, G), :] = whole[:, t * 128 : (t + 1) * 128]
-
-    def mirror_copy(part):
-        strips = (pl.ds(0, 2), pl.ds(2, 3))[part]
-        return pltpu.make_async_remote_copy(
-            src_ref=fold_sum.at[strips, kept],
-            dst_ref=fold_mirror.at[strips, kept],
-            send_sem=send_d.at[3 + part],
-            recv_sem=recv_d.at[3 + part],
-            device_id={"pool": 1 - pool, "pw": mirrors[part]},
-            device_id_type=MESH,
-        )
-
-    for part in range(2):
-        mirror_copy(part).start()
-
-    @pl.loop(0, W - 1, unroll=9)
-    def _(k):
-        peer = peer_at(k)
-        pltpu.make_async_remote_copy(
-            src_ref=spread_out.at[:, peer],
-            dst_ref=spread_in.at[:, me],
-            send_sem=send_d.at[5],
-            recv_sem=recv_d.at[5],
-            device_id={"pw": peer},
-            device_id_type=MESH,
-        ).start()
-
+    spread(R - 1)
     pltpu.make_async_copy(spread_out.at[:, me], spread_in.at[:, me], load_sem.at[12]).start()
 
     wait_bytes(row_in.at[others], recv_r.at[2, 0])
@@ -525,10 +536,11 @@
     own_r(1).wait()
     update(1)
 
-    wait_bytes(spread_in.at[:, others], recv_d.at[5])
+    for j in range(R):
+        wait_bytes(piece_d(spread_in, j, others), recv_d.at[6 + j])
     pltpu.make_async_copy(spread_out.at[:, me], spread_in.at[:, me], load_sem.at[12]).wait()
-    for part in range(2):
-        mirror_copy(part).wait()
+    for j in range(R):
+        mirror_copy(j, kept).wait()
     own = [fold_sum_rows[pl.ds(t * H, H), :] for t in range(5)]
     seen = [fold_mirror_rows[pl.ds(t * H, H), :] for t in range(5)]
     ends = own[4] + swap64(seen[4])
@@ -557,7 +569,8 @@
     wait_bytes(piece_a(out_a, 1, 0, others), send_a.at[1, 0])
     wait_bytes(piece_r(out_r, 0, 0, others), send_r.at[0, 0])
     wait_bytes(row_in.at[others], send_r.at[2, 0])
-    wait_bytes(spread_out.at[:, others], send_d.at[5])
+    for j in range(R):
+        wait_bytes(piece_d(spread_out, j, others), send_d.at[6 + j])
 
 
 def in_hbm(array):
@@ -605,8 +618,8 @@
             dma((4, R)),
             dma((3, R)),
             dma((3, R)),
-            dma((6,)),
-            dma((6,)),
+            dma((9,)),
+            dma((9,)),
         ],
         compiler_params=pltpu.CompilerParams(
             collective_id=0, has_side_effects=True, vmem_limit_bytes=56 * 2**20

time: 92.2 us -> 90.6 us (0.983)
  Pallas kernels: 88.6 us -> 86.5 us
    pallas_call x1, Pallas kernels: 88.6 us -> 86.5 us  [body(): pl.pallas_call(kernel, out_shape=(pltpu.VMEM((1, 2, 2, R, G, G), F32), pl...]
where the time goes in v4:
time: 90.6 us; the launch traced here: 90 us
  Pallas kernels  86.5 us (95%)
  local copies, waits for them, and re-layouts  2.22 us (2%)
  between operations  1.29 us (1%)
    pallas_call x1, Pallas kernels, body(): pl.pallas_call(kernel, out_shape=(pltpu.VMEM((1, 2, 2, R, G, G), F32), pl...  86.5 us
    unnamed x2, local copies, waits for them, and re-layouts  2.22 us

profile of v4, /device:TPU:1, one launch (start us, length us, event | category | flops | bytes accessed | tf_op | source)
XLA Modules:
  0.0 90.0 jit_solution(14835622174914019572)
XLA Ops:
  1.3 86.5 %shard_map.203 = (f32[1,2,2,3,192,192]{5,4,3,2,1,0:T(8,128)S(1)}, f32[3,192,192]{2,1,0:T(8,128)S(1)}) custom-call(f32[1,2,2,3,192,192]{5,4,3,2,1,0:T(8,128)} %orb_hbm.1, f32[1,2,2,3,192,192]{5,4,3,2,1,0:T(8,128)} %resp_hbm.1, f32[3,192,192]{2,1,0:T(8,128)} %bitcast.2, f32[3,192,192]{2,1,0:T(8,128)} %bitcast.3, f32[1,2]{1,0:T(1,128)} %energies.1, ...), custom_call_target="tpu_custom_call" | custom-call | tf_op jit(solution)/shard_map/pallas_call | solution.py:585
  87.8 1.4 %copy.24 = f32[1,2,2,3,192,192]{5,4,3,2,1,0:T(8,128)} copy(f32[1,2,2,3,192,192]{5,4,3,2,1,0:T(8,128)S(1)} %get-tuple-element.2) | data formatting | bytes 3538944
  89.2 0.8 copy.25

commit v5 on v4

--- a/solution.py
+++ b/solution.py
@@ -573,6 +573,19 @@
         wait_bytes(piece_d(spread_out, j, others), send_d.at[6 + j])
 
 
+def store(new_vmem, dens_vmem, new_hbm, dens_hbm, sem):
+    copies = [
+        pltpu.make_async_copy(new_vmem.at[0, n, c], new_hbm.at[0, n, c], sem.at[2 * n + c])
+        for n in range(2)
+        for c in range(2)
+    ]
+    copies.append(pltpu.make_async_copy(dens_vmem, dens_hbm, sem.at[4]))
+    for copy in copies:
+        copy.start()
+    for copy in copies:
+        copy.wait()
+
+
 def in_hbm(array):
     return pltpu.with_memory_space_constraint(array, pltpu.HBM)
 
@@ -582,7 +595,7 @@
     anywhere = pl.BlockSpec(memory_space=pl.ANY)
     scalar = pl.BlockSpec(memory_space=pltpu.SMEM)
     vmem, dma = pltpu.VMEM, pltpu.SemaphoreType.DMA
-    return pl.pallas_call(
+    results = pl.pallas_call(
         kernel,
         out_shape=(
             pltpu.VMEM((1, 2, 2, R, G, G), F32),
@@ -633,6 +646,16 @@
         weights,
         *held,
     )
+    return pl.pallas_call(
+        store,
+        out_shape=(
+            jax.ShapeDtypeStruct((1, 2, 2, R, G, G), F32),
+            jax.ShapeDtypeStruct((R, G, G), F32),
+        ),
+        in_specs=[pl.BlockSpec(memory_space=pltpu.VMEM)] * 2,
+        out_specs=(anywhere, anywhere),
+        scratch_shapes=[dma((5,))],
+    )(*(pltpu.with_memory_space_constraint(result, pltpu.VMEM) for result in results))
 
 
 def solution(mesh):

time: 90.6 us -> 90.1 us (level)
  local copies, waits for them, and re-layouts: 2.22 us -> 0 us
  Pallas kernels: 86.5 us -> 88.1 us
    unnamed x2 -> x0, local copies, waits for them, and re-layouts: 2.22 us -> none
    pallas_call x0 -> x1, Pallas kernels: none -> 1.64 us  [body(): pl.pallas_call(store, out_shape=(jax.ShapeDtypeStruct((1, 2, 2, R, G, G),...]
where the time goes in v5:
time: 90.1 us; the launch traced here: 89.4 us
  Pallas kernels  88.1 us (98%)
  between operations  1.28 us (1%)
    pallas_call x1, Pallas kernels, body(): pl.pallas_call(kernel, out_shape=(pltpu.VMEM((1, 2, 2, R, G, G), F32), pl...  86.5 us

profile of v5, /device:TPU:1, one launch (start us, length us, event | category | flops | bytes accessed | tf_op | source)
XLA Modules:
  0.0 89.4 jit_solution(10555414244765652749)
XLA Ops:
  1.3 86.5 %shard_map.203 = (f32[1,2,2,3,192,192]{5,4,3,2,1,0:T(8,128)S(1)}, f32[3,192,192]{2,1,0:T(8,128)S(1)}) custom-call(f32[1,2,2,3,192,192]{5,4,3,2,1,0:T(8,128)} %orb_hbm.1, f32[1,2,2,3,192,192]{5,4,3,2,1,0:T(8,128)} %resp_hbm.1, f32[3,192,192]{2,1,0:T(8,128)} %bitcast.2, f32[3,192,192]{2,1,0:T(8,128)} %bitcast.3, f32[1,2]{1,0:T(1,128)} %energies.1, ...), custom_call_target="tpu_custom_call" | custom-call | tf_op jit(solution)/shard_map/pallas_call | solution.py:598
  87.8 1.6 %shard_map.204 = (f32[1,2,2,3,192,192]{5,4,3,2,1,0:T(8,128)}, f32[3,192,192]{2,1,0:T(8,128)}) custom-call(f32[1,2,2,3,192,192]{5,4,3,2,1,0:T(8,128)S(1)} %get-tuple-element.4.new_vmem, f32[3,192,192]{2,1,0:T(8,128)S(1)} %get-tuple-element.5.dens_vmem), custom_call_target="tpu_custom_call" | custom-call | tf_op jit(solution)/shard_map/pallas_call | solution.py:649

commit v6 on v5

--- a/solution.py
+++ b/solution.py
@@ -474,9 +474,6 @@
             for k in range(9):
                 send_piece_r(1, j, peer_at(c * 9 + k))
 
-        if j > 0:
-            spread(j - 1)
-
     own_r(1).start()
     row = jnp.zeros((1, 128), F32)
     for k in range(8):
@@ -496,7 +493,8 @@
             device_id_type=MESH,
         ).start()
 
-    spread(R - 1)
+    for j in range(R):
+        spread(j)
     pltpu.make_async_copy(spread_out.at[:, me], spread_in.at[:, me], load_sem.at[12]).start()
 
     wait_bytes(row_in.at[others], recv_r.at[2, 0])

time: 90.1 us -> 88.8 us (0.986)
  no operation moved by 1% of the time
where the time goes in v6:
time: 88.8 us; the launch traced here: 88.6 us
  Pallas kernels  87.4 us (98%)
  between operations  1.28 us (1%)
    pallas_call x1, Pallas kernels, body(): pl.pallas_call(kernel, out_shape=(pltpu.VMEM((1, 2, 2, R, G, G), F32), pl...  85.7 us

profile of v6, /device:TPU:1, one launch (start us, length us, event | category | flops | bytes accessed | tf_op | source)
XLA Modules:
  0.0 88.6 jit_solution(15662525398525543133)
XLA Ops:
  1.3 85.7 %shard_map.203 = (f32[1,2,2,3,192,192]{5,4,3,2,1,0:T(8,128)S(1)}, f32[3,192,192]{2,1,0:T(8,128)S(1)}) custom-call(f32[1,2,2,3,192,192]{5,4,3,2,1,0:T(8,128)} %orb_hbm.1, f32[1,2,2,3,192,192]{5,4,3,2,1,0:T(8,128)} %resp_hbm.1, f32[3,192,192]{2,1,0:T(8,128)} %bitcast.2, f32[3,192,192]{2,1,0:T(8,128)} %bitcast.3, f32[1,2]{1,0:T(1,128)} %energies.1, ...), custom_call_target="tpu_custom_call" | custom-call | tf_op jit(solution)/shard_map/pallas_call | solution.py:596
  87.0 1.6 %shard_map.204 = (f32[1,2,2,3,192,192]{5,4,3,2,1,0:T(8,128)}, f32[3,192,192]{2,1,0:T(8,128)}) custom-call(f32[1,2,2,3,192,192]{5,4,3,2,1,0:T(8,128)S(1)} %get-tuple-element.4.new_vmem, f32[3,192,192]{2,1,0:T(8,128)S(1)} %get-tuple-element.5.dens_vmem), custom_call_target="tpu_custom_call" | custom-call | tf_op jit(solution)/shard_map/pallas_call | solution.py:647

commit v7 on v6

--- a/solution.py
+++ b/solution.py
@@ -418,10 +418,6 @@
             device_id_type=MESH,
         )
 
-    def piece_d(ref, j, who):
-        first, count = strips_of[j]
-        return ref.at[pl.ds(3 * first, 3 * count), who]
-
     def spread(j):
         first, count = strips_of[j]
         pool_copy(j, kept).wait()
@@ -434,20 +430,6 @@
         whole = exact_left(unfold[...], jnp.concatenate(summed, axis=1))
         for t in range(count):
             spread_out_rows[pl.ds((first + t) * G, G), :] = whole[:, t * 128 : (t + 1) * 128]
-
-        @pl.loop(0, 7)
-        def _(c):
-            mirror_copy(j, pl.ds(c * C, C)).start()
-            for k in range(9):
-                peer = peer_at(c * 9 + k)
-                pltpu.make_async_remote_copy(
-                    src_ref=piece_d(spread_out, j, peer),
-                    dst_ref=piece_d(spread_in, j, me),
-                    send_sem=send_d.at[6 + j],
-                    recv_sem=recv_d.at[6 + j],
-                    device_id={"pw": peer},
-                    device_id_type=MESH,
-                ).start()
 
     lane = lax.broadcasted_iota(jnp.int32, (1, 128), 1)
     for j in range(R):
@@ -495,6 +477,22 @@
 
     for j in range(R):
         spread(j)
+
+    @pl.loop(0, 7)
+    def _(c):
+        for j in range(R):
+            mirror_copy(j, pl.ds(c * C, C)).start()
+        for k in range(9):
+            peer = peer_at(c * 9 + k)
+            pltpu.make_async_remote_copy(
+                src_ref=spread_out.at[:, peer],
+                dst_ref=spread_in.at[:, me],
+                send_sem=send_d.at[6],
+                recv_sem=recv_d.at[6],
+                device_id={"pw": peer},
+                device_id_type=MESH,
+            ).start()
+
     pltpu.make_async_copy(spread_out.at[:, me], spread_in.at[:, me], load_sem.at[12]).start()
 
     wait_bytes(row_in.at[others], recv_r.at[2, 0])
@@ -534,8 +532,7 @@
     own_r(1).wait()
     update(1)
 
-    for j in range(R):
-        wait_bytes(piece_d(spread_in, j, others), recv_d.at[6 + j])
+    wait_bytes(spread_in.at[:, others], recv_d.at[6])
     pltpu.make_async_copy(spread_out.at[:, me], spread_in.at[:, me], load_sem.at[12]).wait()
     for j in range(R):
         mirror_copy(j, kept).wait()
@@ -567,8 +564,7 @@
     wait_bytes(piece_a(out_a, 1, 0, others), send_a.at[1, 0])
     wait_bytes(piece_r(out_r, 0, 0, others), send_r.at[0, 0])
     wait_bytes(row_in.at[others], send_r.at[2, 0])
-    for j in range(R):
-        wait_bytes(piece_d(spread_out, j, others), send_d.at[6 + j])
+    wait_bytes(spread_out.at[:, others], send_d.at[6])
 
 
 def store(new_vmem, dens_vmem, new_hbm, dens_hbm, sem):
@@ -629,8 +625,8 @@
             dma((4, R)),
             dma((3, R)),
             dma((3, R)),
-            dma((9,)),
-            dma((9,)),
+            dma((7,)),
+            dma((7,)),
         ],
         compiler_params=pltpu.CompilerParams(
             collective_id=0, has_side_effects=True, vmem_limit_bytes=56 * 2**20

time: 88.8 us -> 91.9 us (1.035)
  Pallas kernels: 87.4 us -> 90.4 us
    pallas_call x1, Pallas kernels: 85.7 us -> 88.8 us  [body(): pl.pallas_call(kernel, out_shape=(pltpu.VMEM((1, 2, 2, R, G, G), F32), pl...]
where the time goes in v7:
time: 91.9 us; the launch traced here: 91.7 us
  Pallas kernels  90.4 us (98%)
  between operations  1.28 us (1%)
    pallas_call x1, Pallas kernels, body(): pl.pallas_call(kernel, out_shape=(pltpu.VMEM((1, 2, 2, R, G, G), F32), pl...  88.8 us

profile of v7, /device:TPU:1, one launch (start us, length us, event | category | flops | bytes accessed | tf_op | source)
XLA Modules:
  0.0 91.7 jit_solution(10898631449502798640)
XLA Ops:
  1.3 88.8 %shard_map.203 = (f32[1,2,2,3,192,192]{5,4,3,2,1,0:T(8,128)S(1)}, f32[3,192,192]{2,1,0:T(8,128)S(1)}) custom-call(f32[1,2,2,3,192,192]{5,4,3,2,1,0:T(8,128)} %orb_hbm.1, f32[1,2,2,3,192,192]{5,4,3,2,1,0:T(8,128)} %resp_hbm.1, f32[3,192,192]{2,1,0:T(8,128)} %bitcast.2, f32[3,192,192]{2,1,0:T(8,128)} %bitcast.3, f32[1,2]{1,0:T(1,128)} %energies.1, ...), custom_call_target="tpu_custom_call" | custom-call | tf_op jit(solution)/shard_map/pallas_call | solution.py:592
  90.1 1.6 %shard_map.204 = (f32[1,2,2,3,192,192]{5,4,3,2,1,0:T(8,128)}, f32[3,192,192]{2,1,0:T(8,128)}) custom-call(f32[1,2,2,3,192,192]{5,4,3,2,1,0:T(8,128)S(1)} %get-tuple-element.4.new_vmem, f32[3,192,192]{2,1,0:T(8,128)S(1)} %get-tuple-element.5.dens_vmem), custom_call_target="tpu_custom_call" | custom-call | tf_op jit(solution)/shard_map/pallas_call | solution.py:643
